TPU v7x, 128 devices: a whole 4x4x4 slice. The times are simulated.
128 devices in a mesh: batch: 8 (over y_hi, x), task: 16 (over y_lo, z, core).
Axes of the slice: x: 4, y: 4 (y_hi: 2, y_lo: 2; y = y_hi * 2 + y_lo), z: 4, core: 2. Of those that a mesh axis runs over, the one named last changes fastest.
Arguments:
- x_quant: bfloat16 [4096, 4096], P('batch', 'task'), may hold values from -6 to 6
- x_scale: bfloat16 [4096, 32], P('batch', 'task'), may hold values from 0.25 to 2.5
- user_feats: bfloat16 [4096, 384], P('batch'), may hold values from -6 to 6
- scenario_ids: int32 [4096], P('batch'), may hold values from 0 to 31
- scenario_table: bfloat16 [32, 128], replicated, may hold values from -6 to 6
- label_mask: int32 [4096, 16], P('batch', 'task'), may hold values 0 or 1
- saved_z: bfloat16 [16, 4096, 2048], P('task', 'batch'), may hold values from -6 to 6
- out_grad: bfloat16 [16, 4096, 2048], P('task', 'batch'), may hold values from -4 to 4
- main_weight: bfloat16 [16, 4096, 2048], P('task'), may hold values from -0.09375 to 0.09375
- gate_a: bfloat16 [16, 512, 512], P('task'), may hold values from -0.25 to 0.25
- gate_b: bfloat16 [16, 512, 2048], P('task'), may hold values from -0.25 to 0.25
Outputs:
- main_grad: bfloat16 [16, 4096, 2048], P('task', 'batch')
- gate_a_grad: bfloat16 [16, 512, 512], P('task', 'batch')
- gate_b_grad: bfloat16 [16, 512, 2048], P('task', 'batch')
- x_grad: bfloat16 [4096, 4096], P('batch', 'task')
- user_grad: bfloat16 [4096, 384], P('batch', 'task')
- table_grad: float32 [32, 128], replicated
All inputs are finite; a program needn't handle non-finite values. No bound on the sum of `label_mask` on one device may be relied on, other than what follows from the above.
Results may differ from a plain program's by a relative error of at most 0.02.
Values may be sent and summed in bfloat16 or wider, within the bound.
A program may use at most 192 MiB of HBM per device.

v0:
```python
import jax
import jax.numpy as jnp
from jax import lax
from jax.sharding import PartitionSpec as P


def dequantize(values, scales):
    row_count, width = values.shape
    blocks = scales.shape[1]
    grid = (
        values.astype(jnp.float32).reshape(row_count, blocks, width // blocks)
        * scales.astype(jnp.float32)[:, :, None]
    )
    return grid.reshape(row_count, width).astype(jnp.bfloat16)


def body(
    x_quant,
    x_scale,
    user_feats,
    scenario_ids,
    scenario_table,
    label_mask,
    saved_z,
    out_grad,
    main_weight,
    gate_a,
    gate_b,
):
    weight = main_weight[0]
    weight_a = gate_a[0]
    weight_b = gate_b[0]
    user_width = user_feats.shape[1]
    categories = scenario_table.shape[0]
    onehot = (scenario_ids[:, None] == jnp.arange(categories, dtype=jnp.int32)[None, :]).astype(
        jnp.bfloat16
    )
    scen_rows = jnp.dot(onehot, scenario_table, preferred_element_type=jnp.float32).astype(
        jnp.bfloat16
    )
    gate_in = jnp.concatenate([user_feats, scen_rows], axis=1)
    a_pre = jnp.dot(gate_in, weight_a, preferred_element_type=jnp.float32)
    a_act = jnp.maximum(a_pre, 0.0).astype(jnp.bfloat16)
    gate_value = 2.0 * jax.nn.sigmoid(jnp.dot(a_act, weight_b, preferred_element_type=jnp.float32))
    masked = out_grad[0].astype(jnp.float32) * label_mask.astype(jnp.float32)
    preact = saved_z[0].astype(jnp.float32)
    z_grad = (masked * gate_value * (preact > 0)).astype(jnp.bfloat16)
    u_grad = (masked * jnp.maximum(preact, 0.0) * gate_value * (1.0 - 0.5 * gate_value)).astype(
        jnp.bfloat16
    )
    a_back = jnp.einsum("rh,gh->rg", u_grad, weight_b, preferred_element_type=jnp.float32)
    a_grad = (a_back * (a_pre > 0)).astype(jnp.bfloat16)
    gin_grad = jnp.einsum("rg,ig->ri", a_grad, weight_a, preferred_element_type=jnp.float32)
    partial_a = jnp.einsum("ri,rg->ig", gate_in, a_grad, preferred_element_type=jnp.float32)
    partial_b = jnp.einsum("rg,rh->gh", a_act, u_grad, preferred_element_type=jnp.float32)
    grad_a, grad_b = (
        lax.psum_scatter(
            partial_a.astype(jnp.bfloat16), "batch", scatter_dimension=0, tiled=True
        ).astype(jnp.float32),
        lax.psum_scatter(
            partial_b.astype(jnp.bfloat16), "batch", scatter_dimension=0, tiled=True
        ).astype(jnp.float32),
    )
    quant_all, scale_all = (
        lax.all_gather(x_quant, "task", axis=1, tiled=True),
        lax.all_gather(x_scale, "task", axis=1, tiled=True),
    )
    inputs = dequantize(quant_all, scale_all)
    main_sum = lax.psum_scatter(
        jnp.einsum("rd,rh->dh", inputs, z_grad, preferred_element_type=jnp.float32).astype(
            jnp.bfloat16
        ),
        "batch",
        scatter_dimension=0,
        tiled=True,
    )
    x_local = jnp.einsum("rh,dh->rd", z_grad, weight, preferred_element_type=jnp.float32)
    onehot_wide = onehot.astype(jnp.float32)
    x_part, user_part = (
        lax.psum_scatter(
            x_local.astype(jnp.bfloat16), "task", scatter_dimension=1, tiled=True
        ).astype(jnp.float32),
        lax.psum_scatter(
            gin_grad[:, :user_width].astype(jnp.bfloat16), "task", scatter_dimension=1, tiled=True
        ).astype(jnp.float32),
    )
    table_local = jnp.einsum(
        "rc,rs->cs", onehot_wide, gin_grad[:, user_width:], precision=lax.Precision.HIGHEST
    )
    table_grad = lax.psum(table_local, ("batch", "task"))
    return (
        main_sum[None],
        grad_a.astype(jnp.bfloat16)[None],
        grad_b.astype(jnp.bfloat16)[None],
        x_part.astype(jnp.bfloat16),
        user_part.astype(jnp.bfloat16),
        table_grad,
    )


def solution(mesh):
    placed = (
        P("batch", "task"),
        P("batch", "task"),
        P("batch", None),
        P("batch"),
        P(),
        P("batch", "task"),
        P("task", "batch", None),
        P("task", "batch", None),
        P("task", None, None),
        P("task", None, None),
        P("task", None, None),
    )
    return jax.shard_map(
        body,
        mesh=mesh,
        in_specs=placed,
        out_specs=(
            P("task", "batch", None),
            P("task", "batch", None),
            P("task", "batch", None),
            P("batch", "task"),
            P("batch", "task"),
            P(),
        ),
        check_vma=False,
    )
```

profile of v0, /device:TPU:8, one launch (start us, length us, event | category | flops | bytes accessed | tf_op | source)
XLA Modules:
  0.0 545.1 jit_solution(12517591365654852456)
XLA Ops:
  7.2 0.7 all-gather.3.cloned.1.call-update
  8.0 1.0 convolution_convert_fusion.3
  9.1 0.7 convert_element_type.68
  9.8 1.6 fusion.27
  11.4 6.1 %fusion.10 = (bf16[512,2048]{1,0:T(8,128)(2,1)S(1)}, bf16[512,2048]{1,0:T(8,128)(2,1)}) fusion(bf16[1,512,2048]{2,1,0:T(8,128)(2,1)} %param.17, bf16[1,512,2048]{2,1,0:T(8,128)(2,1)} %param.18, f32[512]{0:T(512)S(1)} %bitcast.66, bf16[1,512,2048]{2,1,0:T(8,128)(2,1)S(1)} %copy-done, f32[512,512]{1,0:T(8,128)S(1)} %fusion.27), kind=kOutput, calls=%fused_computation.12 | convolution fusion | flops 1092091904 | bytes 11536384 | tf_op jit(solution)/shard_map/dot_general | solution.py:44
  17.5 1.4 fusion.22
  18.9 0.5 fusion.25
  19.4 0.3 copy-done.5
  19.8 0.9 copy.23
  20.8 2.4 convolution_convert_fusion.2
  23.3 4.2 convolution_convert_fusion.1
  27.6 14.5 %fusion.3 = bf16[512,4096]{1,0:T(8,128)(2,1)} fusion(bf16[512,2048]{1,0:T(8,128)(2,1)} %get-tuple-element.19, bf16[1,4096,2048]{2,1,0:T(8,128)(2,1)} %param.19), kind=kOutput, calls=%fused_computation.5 | convolution fusion | flops 8592031744 | bytes 23068672 | tf_op jit(solution)/shard_map/rh,dh->rd/dot_general | solution.py:77
  42.2 0.6 copy-done.7
  42.8 20.0 %all-gather = bf16[16,2,512]{2,1,0:T(2,128)(2,1)S(1)} all-gather(bf16[1,2,512]{2,1,0:T(2,128)(2,1)S(1)} %bitcast.65), channel_id=1, replica_groups=mesh['batch'=8,'task'=16] {'task'}, dimensions={0}, use_global_device_ids=true | all-gather | bytes 34816 | tf_op jit(solution)/shard_map/all_gather | solution.py:66
  62.8 0.1 copy.20
  63.0 5.8 %mul.47 = f32[512,32,128]{2,1,0:T(8,128)} broadcast(f32[512,32]{1,0:T(8,128)S(1)} %copy.20), dimensions={0,1} | broadcast | bytes 8454144 | tf_op jit(solution)/shard_map/mul | solution.py:11
  68.7 32.0 %convolution_convert_fusion = bf16[4096,2048]{1,0:T(8,128)(2,1)} fusion(bf16[512,2048]{1,0:T(8,128)(2,1)} %get-tuple-element.19, f32[64,8,32,128]{3,2,1,0:T(8,128)} %bitcast.62, bf16[512,4096]{1,0:T(8,128)(2,1)} %all-gather.3.cloned.1.call-done), kind=kOutput, calls=%fused_computation.2 | convolution fusion | flops 8604614656 | bytes 31457280 | tf_op jit(solution)/shard_map/rd,rh->dh/dot_general | solution.py:70
  100.8 0.7 copy-done.6
  101.4 0.4 fusion.29
  101.9 66.2 %psum.7 = f32[32,128]{1,0:T(8,128)} all-reduce(f32[32,128]{1,0:T(8,128)S(1)} %fusion.29), channel_id=1, replica_groups=mesh['batch'=8,'task'=16] {'batch','task'}, use_global_device_ids=true, to_apply=%region_5.0 | all-reduce | flops 4096 | bytes 32768 | tf_op jit(solution)/shard_map/psum | solution.py:90
  168.1 25.9 %reduce-scatter.10.cloned.1.call-done = bf16[64,512]{1,0:T(8,128)(2,1)} async-done(((bf16[512,512]{1,0:T(8,128)(2,1)}), bf16[64,512]{1,0:T(8,128)(2,1)}) %reduce-scatter.10.cloned.1.call-update) | async-done | bytes 65552 | tf_op jit(solution)/shard_map/reduce_scatter | solution.py:57
  193.9 78.4 %reduce-scatter.12.cloned.1.call-done = bf16[64,2048]{1,0:T(8,128)(2,1)} async-done(((bf16[512,2048]{1,0:T(8,128)(2,1)}), bf16[64,2048]{1,0:T(8,128)(2,1)}) %reduce-scatter.12.cloned.1.call-update) | async-done | bytes 262160 | tf_op jit(solution)/shard_map/reduce_scatter | solution.py:60
  272.4 68.6 %reduce-scatter.14.cloned.1.call-done = bf16[512,256]{1,0:T(8,128)(2,1)} async-done(((bf16[512,4096]{1,0:T(8,128)(2,1)}), bf16[512,256]{1,0:T(8,128)(2,1)}) %reduce-scatter.14.cloned.1.call-update) | async-done | bytes 262160 | tf_op jit(solution)/shard_map/reduce_scatter | solution.py:80
  341.0 197.2 %reduce-scatter.8.cloned.1.call-done = bf16[512,2048]{1,0:T(8,128)(2,1)} async-done(((bf16[4096,2048]{1,0:T(8,128)(2,1)}), bf16[512,2048]{1,0:T(8,128)(2,1)}) %reduce-scatter.8.cloned.1.call-update) | async-done | bytes 2097168 | tf_op jit(solution)/shard_map/reduce_scatter | solution.py:69
  (31 shorter events, 0.6 us)
Async XLA Ops:
  7.2 4.2 copy-start
  7.2 55.8 %all-gather.3.cloned.1.call-start = ((), (), s32[]{:S(2)}) async-start(), calls=%async_computation.5 | async-start | bytes 4456448 | tf_op jit(solution)/shard_map/all_gather | solution.py:65
  7.9 160.2 %reduce-scatter.16.cloned.1.call-start = ((), (), s32[]{:S(2)}) async-start(), calls=%async_computation.10 | async-start | bytes 417792
  11.4 6.1 %copy-start.3 = (f32[512,512]{1,0:T(8,128)}, f32[512,512]{1,0:T(8,128)S(1)}, u32[]{:S(2)}) copy-start(f32[512,512]{1,0:T(8,128)S(1)} %fusion.27) | copy-start | bytes 3145732
  17.5 1.4 copy-start.8
  17.5 1.4 copy-start.2
  18.9 0.8 copy-start.5
  18.9 4.4 copy-start.4
  20.7 173.2 %reduce-scatter.10.cloned.1.call-start = ((), (), s32[]{:S(2)}) async-start(), calls=%async_computation.7 | async-start | bytes 589824 | tf_op jit(solution)/shard_map/reduce_scatter | solution.py:57
  23.3 249.1 %reduce-scatter.12.cloned.1.call-start = ((), (), s32[]{:S(2)}) async-start(), calls=%async_computation.8 | async-start | bytes 2359296 | tf_op jit(solution)/shard_map/reduce_scatter | solution.py:60
  27.6 313.5 %reduce-scatter.14.cloned.1.call-start = ((), (), s32[]{:S(2)}) async-start(), calls=%async_computation.9 | async-start | bytes 4456448 | tf_op jit(solution)/shard_map/reduce_scatter | solution.py:80
  42.1 0.7 copy-start.7
  42.1 496.1 %reduce-scatter.8.cloned.1.call-start = ((), (), s32[]{:S(2)}) async-start(), calls=%async_computation.6 | async-start | bytes 18874368 | tf_op jit(solution)/shard_map/reduce_scatter | solution.py:69
  100.7 0.7 copy-start.6
  101.4 436.8 %copy-start.1 = (bf16[1,512,2048]{2,1,0:T(8,128)(2,1)S(1)}, bf16[1,512,2048]{2,1,0:T(8,128)(2,1)}, u32[]{:S(2)}) copy-start(bf16[1,512,2048]{2,1,0:T(8,128)(2,1)} %param.21) | copy-start | bytes 6291460
Sparse Core Ops, SparseCore 0:
  9.6 47.2 all-gather.2
  59.9 60.0 reduce-scatter.15
  124.6 69.2 reduce-scatter.9
  198.1 74.1 reduce-scatter.11
  275.3 65.6 reduce-scatter.13
  345.9 192.2 reduce-scatter.7
where the time goes:
time: 546 us; the launch traced here: 545 us
  waiting for transfers between devices  371 us (68%)
  blocking collectives  86.2 us (16%)
  matrix products  64.1 us (12%)
  between operations  14.2 us (3%)
  local copies, waits for them, and re-layouts  8.61 us (2%)
    reduce_scatter x1, waiting for transfers between devices, body(): lax.psum_scatter(jnp.einsum('rd,rh->dh', inputs, z_grad, preferred_elemen...  197 us
    reduce_scatter x1, waiting for transfers between devices, body(): lax.psum_scatter(partial_b.astype(jnp.bfloat16), 'batch', scatter_dimensi...  78.4 us
    reduce_scatter x1, waiting for transfers between devices, body(): lax.psum_scatter(x_local.astype(jnp.bfloat16), 'task', scatter_dimension=...  68.6 us
    psum x1, blocking collectives, body(): table_grad = lax.psum(table_local, ('batch', 'task'))  66.2 us
    dot_general x1, matrix products, body(): jnp.einsum('rd,rh->dh', inputs, z_grad, preferred_element_type=jnp.float32)  32 us
    reduce_scatter x1, waiting for transfers between devices, body(): lax.psum_scatter(partial_a.astype(jnp.bfloat16), 'batch', scatter_dimensi...  25.9 us
    all_gather x1, blocking collectives, body(): lax.all_gather(x_scale, 'task', axis=1, tiled=True)  20 us
    dot_general x1, matrix products, body(): jnp.einsum('rh,dh->rd', z_grad, weight, preferred_element_type=jnp.float32)  14.5 us
  transfers between devices with their start and end apart: 6, of which 4 were waited for; matrix products, arithmetic and copies ran while one was open for 13% of the time, Pallas kernels for 0%

commit v1 on v0

v1 whole, which is shorter than its diff:
```python
import jax
import jax.numpy as jnp
from jax import lax
from jax.experimental import pallas as pl
from jax.experimental.pallas import tpu as pltpu
from jax.sharding import PartitionSpec as P

MESH = pl.DeviceIdType.MESH
F32 = jnp.float32
BF16 = jnp.bfloat16

ROWS = 512
H = 2048
GH = 512
UD = 384
CH = 256
STEPS = H // CH
XB = 288
USER = 24

Z_Y, Z_E0, Z_FW = 0, 8, 16
G_E1, G_Y, G_E0 = 24, 33, 34
I_PERM, I_YL, I_Z1, I_Z2, I_CORE = 35, 36, 37, 39, 41
M_E1 = 45
X_CORE, X_Z1, X_Z2, X_YL = 53, 61, 63, 67
T_ALL = 68
N_SEM = 75


def nt(a, b):
    return lax.dot_general(a, b, (((1,), (1,)), ((), ())), preferred_element_type=F32)


def nn(a, b):
    return jnp.dot(a, b, preferred_element_type=F32)


def kernel(
    xq, xs, feats, ids_col, ids_row, table, mask_col, ga, gb, sz_hbm, og_hbm, w_hbm,
    main_out, ga_out, gb_out, x_out, user_out, table_out,
    sz, og, wbuf, zall, gin_in, act, a_back, gint, aall, x_own,
    gpart, gr1, gr2, gr3, xsend, xkeep, xcore, xz1, xz2, xylsend, xyl, ps, pr, tsend, trecv,
    lsem, ssem, rsem,
):
    bi = lax.axis_index("batch")
    ti = lax.axis_index("task")
    yh, x = bi // 4, bi % 4
    yl, z, c = ti // 8, (ti // 2) % 4, ti % 2
    x0 = x + 1 - 2 * (x % 2)
    x1 = 3 - x
    xp = x // 2
    z0 = z + 1 - 2 * (z % 2)

    def dev(yh_, x_, yl_, z_, c_):
        return (yh_ * 4 + x_, yl_ * 8 + z_ * 2 + c_)

    d_y = dev(1 - yh, x, yl, z, c)
    d_e0 = dev(yh, x0, yl, z, c)
    d_e1 = dev(yh, x1, yl, z, c)
    d_c = dev(yh, x, yl, z, 1 - c)
    d_yl = dev(yh, x, 1 - yl, z, c)
    d_zp = dev(yh, x, yl, (z + 1) % 4, c)
    d_zm = dev(yh, x, yl, (z + 3) % 4, c)
    member = jnp.logical_or(z == x, z == 3 - x)
    ksel = jnp.where(member, 0, 1)
    is_self = jnp.logical_and(member, yh == yl)
    d_perm = dev(yl, x + ksel * (x0 - x), yh, z + ksel * (z0 - z), c)

    def rcopy(src, dst, i, target):
        return pltpu.make_async_remote_copy(
            src_ref=src, dst_ref=dst, send_sem=ssem.at[i], recv_sem=rsem.at[i],
            device_id=target, device_id_type=MESH)

    def send(src, dst, i, target):
        rcopy(src, dst, i, target).start()

    def got(ref, i):
        rcopy(ref, ref, i, d_c).wait_recv()

    def sent(ref, i):
        rcopy(ref, ref, i, d_c).wait_send()

    def cols(k):
        return pl.ds(pl.multiple_of(k * CH, CH), CH)

    def wcopy(k):
        return pltpu.make_async_copy(
            w_hbm.at[pl.ds(pl.multiple_of(k * 512, 512), 512)], wbuf.at[k % 2], lsem.at[2 + k % 2])

    sz_copy = pltpu.make_async_copy(sz_hbm, sz, lsem.at[0])
    og_copy = pltpu.make_async_copy(og_hbm, og, lsem.at[1])
    sz_copy.start()
    og_copy.start()
    wcopy(0).start()
    wcopy(1).start()

    barrier = pltpu.get_barrier_semaphore()
    for target in (d_y, d_e0, d_e1, d_c, d_yl, d_zp, d_zm):
        pl.semaphore_signal(barrier, inc=1, device_id=target, device_id_type=MESH)

    @pl.when(jnp.logical_not(is_self))
    def _():
        pl.semaphore_signal(barrier, inc=1, device_id=d_perm, device_id_type=MESH)

    half = xq.shape[1] // 2
    for j in range(2):
        part = xq[:, j * half:(j + 1) * half].astype(F32) * xs[:, j:j + 1].astype(F32)
        x_own[j * half:(j + 1) * half, :] = part.T.astype(BF16)

    pl.semaphore_wait(barrier, jnp.where(is_self, 7, 8))

    def place(zz, core, first, count):
        d_ = jnp.where(zz // 2 == xp, 1, 0)
        k_ = jnp.where(jnp.logical_or(zz == x, zz == 3 - x), 0, 1)
        off = pl.multiple_of((k_ * 2 + first) * ROWS, ROWS)
        return aall.at[d_, core, :, pl.ds(off, count * ROWS)]

    @pl.when(is_self)
    def _():
        local = pltpu.make_async_copy(x_own, place(z, c, yl, 1), lsem.at[4])
        local.start()
        local.wait()

    @pl.when(jnp.logical_not(is_self))
    def _():
        send(x_own, place(z, c, yh, 1), I_PERM, d_perm)

    onehot = (ids_col[...] == lax.broadcasted_iota(jnp.int32, (ROWS, 32), 1)).astype(BF16)
    gin_in[:, :UD] = feats[...]
    gin_in[:, UD:] = nn(onehot, table[...]).astype(BF16)
    a_pre = nn(gin_in[...], ga[...])
    a_act = jnp.maximum(a_pre, 0.0)
    act[0] = a_act.astype(BF16)
    act[1] = a_act.T.astype(BF16)
    a_back[...] = jnp.zeros_like(a_back)
    mask = mask_col[...].astype(F32)
    sz_copy.wait()
    og_copy.wait()

    def first(k, carry):
        cc = cols(k)
        gate = 2.0 * jax.nn.sigmoid(nn(act[0], gb[:, cc]))
        masked = og[:, cc].astype(F32) * mask
        pre = sz[:, cc].astype(F32)
        mg = masked * gate
        zall[yh, :, cc] = jnp.where(pre > 0, mg, 0.0).astype(BF16)
        send(zall.at[yh, :, cc], zall.at[yh, :, cc], Z_Y + k, d_y)

        @pl.when(k < 4)
        def _():
            send(zall.at[yh, :, cc], zall.at[2 + yh, :, cc], Z_E0 + k, d_e0)

        u = (jnp.maximum(pre, 0.0) * mg * (1.0 - 0.5 * gate)).astype(BF16)
        part = nn(act[1], u).astype(BF16)
        for i in range(2):
            for j in range(2):
                r = (i * 2 + j) * 128
                gpart[i, j, :, cc] = part[r:r + 128]
        send(gpart.at[:, 1 - xp, :, cc], gr1.at[:, :, cc], G_E1 + k, d_e1)
        a_back[...] += nt(u, gb[:, cc])
        return carry

    lax.fori_loop(0, STEPS, first, 0)

    @pl.when(jnp.logical_not(is_self))
    def _():
        got(place(z, c, yl, 1), I_PERM)

    send(place(z, c, yl, 1), place(z, c, yl, 1), I_YL, d_yl)

    a_grad = jnp.where(act[0].astype(F32) > 0, a_back[...], 0.0).astype(BF16)
    part = nn(gin_in[...].astype(F32).T.astype(BF16), a_grad).astype(BF16)
    for i in range(2):
        for j in range(2):
            r = (i * 2 + j) * 128
            gpart[i, j, :, H:] = part[r:r + 128]
    send(gpart.at[:, 1 - xp, :, pl.ds(H, GH)], gr1.at[:, :, pl.ds(H, GH)], G_E1 + 8, d_e1)
    gint[...] = nt(ga[...], a_grad)
    scen = nt(a_grad, ga[UD:, :])
    onehot_t = (ids_row[...] == lax.broadcasted_iota(jnp.int32, (32, ROWS), 0)).astype(F32)
    tsend[0] = lax.dot_general(
        onehot_t, scen, (((1,), (0,)), ((), ())), precision=lax.Precision.HIGHEST, preferred_element_type=F32)
    t_partners = (d_c, d_e0, d_yl, dev(yh, x, yl, z0, c), d_e1, dev(yh, x, yl, 3 - z, c), d_y)
    send(tsend.at[0], trecv.at[0], T_ALL, t_partners[0])

    def user_rows(t):
        rows = gint[pl.ds(pl.multiple_of(t * USER, 8), USER), :]
        return jnp.concatenate([rows, jnp.zeros((XB - 256 - USER, ROWS), F32)], axis=0).astype(BF16)

    def second(k, carry):
        cc = cols(k)
        wcopy(k).wait()
        wrows = wbuf.at[k % 2]
        other = 1 - c
        own_z = zall[yh]
        xsend[k, :256, :] = nt(wrows[pl.ds(pl.multiple_of(other * 256, 256), 256), :], own_z).astype(BF16)
        xsend[k, 256:, :] = user_rows(k * 2 + other)
        send(xsend.at[k], xcore.at[k], X_CORE + k, d_c)
        xkeep[k, :256, :] = nt(wrows[pl.ds(pl.multiple_of(c * 256, 256), 256), :], own_z).astype(BF16)
        xkeep[k, 256:, :] = user_rows(k * 2 + c)

        @pl.when(k < STEPS - 2)
        def _():
            wcopy(k + 2).start()

        got(zall.at[1 - yh, :, cc], Z_Y + k)
        send(zall.at[1 - yh, :, cc], zall.at[3 - yh, :, cc], Z_FW + k, d_e0)

        @pl.when(k < 4)
        def _():
            more = cols(k + 4)
            send(zall.at[yh, :, more], zall.at[2 + yh, :, more], Z_E0 + 4 + k, d_e0)

        for s in range(1, 7):

            @pl.when(k == s)
            def _():
                got(trecv.at[s - 1], T_ALL + s - 1)
                tsend[s] = tsend[s - 1] + trecv[s - 1]
                send(tsend.at[s], trecv.at[s], T_ALL + s, t_partners[s])

        @pl.when(k == 1)
        def _():
            got(place(z, c, 1 - yl, 1), I_YL)
            mine = place(z, c, 0, 2)
            send(mine, mine, I_Z1, d_zp)
            send(mine, mine, I_Z1 + 1, d_zm)
            send(mine, mine, I_CORE, d_c)

        @pl.when(k == 4)
        def _():
            got(place((z + 3) % 4, c, 0, 2), I_Z1)
            got(place((z + 1) % 4, c, 0, 2), I_Z1 + 1)
            low = place((z + 3) % 4, c, 0, 1)
            send(low, low, I_Z2, d_zp)
            high = place((z + 1) % 4, c, 1, 1)
            send(high, high, I_Z2 + 1, d_zm)
            for i, zz in ((1, (z + 3) % 4), (2, (z + 1) % 4)):
                mine = place(zz, c, 0, 2)
                send(mine, mine, I_CORE + i, d_c)

        @pl.when(k == 6)
        def _():
            got(place((z + 2) % 4, c, 0, 1), I_Z2)
            got(place((z + 2) % 4, c, 1, 1), I_Z2 + 1)
            mine = place((z + 2) % 4, c, 0, 2)
            send(mine, mine, I_CORE + 3, d_c)

        return carry

    lax.fori_loop(0, STEPS, second, 0)

    got(trecv.at[6], T_ALL + 6)
    table_out[...] = tsend[6] + trecv[6]

    def core_sum(k, carry):
        got(xcore.at[k], X_CORE + k)
        xkeep[k] = (xkeep[k].astype(F32) + xcore[k].astype(F32)).astype(BF16)
        return carry

    lax.fori_loop(0, STEPS, core_sum, 0)
    zn, zb, zf = (z + 1) % 4, (z + 3) % 4, (z + 2) % 4
    send(xkeep.at[zf], xz1.at[0], X_Z1, d_zp)
    send(xkeep.at[4 + zf], xz1.at[1], X_Z1 + 1, d_zm)

    for k in range(STEPS):
        got(gr1.at[:, :, pl.ds(k * CH, CH)], G_E1 + k)
    got(gr1.at[:, :, pl.ds(H, GH)], G_E1 + 8)
    gpart[1 - yh, xp] = (gpart[1 - yh, xp].astype(F32) + gr1[1 - yh].astype(F32)).astype(BF16)
    send(gpart.at[1 - yh, xp], gr2, G_Y, d_y)

    for i, zz in enumerate((zb, zn, zf)):
        got(place(zz, 1 - c, 0, 2), I_CORE + 1 + i)
    got(place(z, 1 - c, 0, 2), I_CORE)

    def third(k, carry):
        @pl.when(k < STEPS)
        def _():
            cc = cols(k)
            got(zall.at[2 + yh, :, cc], Z_E0 + k)
            got(zall.at[3 - yh, :, cc], Z_FW + k)
            for j in range(2):
                total = nn(aall[0, j, :, 0:ROWS], zall[0, :, cc])
                for s in range(1, 4):
                    total += nn(aall[0, j, :, s * ROWS:(s + 1) * ROWS], zall[s, :, cc])
                ps[j * 256:(j + 1) * 256, cc] = total.astype(BF16)
            send(ps.at[:, cc], pr.at[:, cc], M_E1 + k, d_e1)

        @pl.when(k >= 1)
        def _():
            cc = cols(k - 1)
            got(pr.at[:, cc], M_E1 + k - 1)
            for j in range(2):
                total = pr[j * 256:(j + 1) * 256, cc].astype(F32)
                for s in range(4):
                    total += nn(aall[1, j, :, s * ROWS:(s + 1) * ROWS], zall[s, :, cc])
                main_out[j * 256:(j + 1) * 256, cc] = total.astype(BF16)

        @pl.when(k == 1)
        def _():
            got(xz1.at[0], X_Z1)
            got(xz1.at[1], X_Z1 + 1)
            xkeep[zn] = (xkeep[zn].astype(F32) + xz1[0].astype(F32)).astype(BF16)
            xkeep[4 + zb] = (xkeep[4 + zb].astype(F32) + xz1[1].astype(F32)).astype(BF16)
            for h in range(2):
                send(xkeep.at[h * 4 + zn], xz2.at[0, h], X_Z2 + 2 * h, d_zp)
                send(xkeep.at[h * 4 + zb], xz2.at[1, h], X_Z2 + 1 + 2 * h, d_zm)

        @pl.when(k == 2)
        def _():
            got(gr2, G_Y)
            gpart[yh, xp] = (
                gpart[yh, xp].astype(F32) + gr1[yh].astype(F32) + gr2[...].astype(F32)).astype(BF16)
            far = pl.ds(pl.multiple_of((x0 % 2) * 64, 64), 64)
            send(gpart.at[yh, xp, far], gr3, G_E0, d_e0)

        @pl.when(k == 4)
        def _():
            for h in range(2):
                got(xz2.at[0, h], X_Z2 + 2 * h)
                got(xz2.at[1, h], X_Z2 + 1 + 2 * h)
            xylsend[...] = (
                xkeep[(1 - yl) * 4 + z].astype(F32) + xz2[0, 1 - yl].astype(F32) + xz2[1, 1 - yl].astype(F32)
            ).astype(BF16)
            send(xylsend, xyl, X_YL, d_yl)

        @pl.when(k == 6)
        def _():
            got(gr3, G_E0)
            near = pl.ds(pl.multiple_of((x % 2) * 64, 64), 64)
            total = gpart[yh, xp, near, :].astype(F32) + gr3[...].astype(F32)
            gb_out[...] = total[:, :H].astype(BF16)
            ga_out[...] = total[:, H:].astype(BF16)

        @pl.when(k == 7)
        def _():
            got(xyl, X_YL)
            total = (
                xkeep[yl * 4 + z].astype(F32) + xz2[0, yl].astype(F32) + xz2[1, yl].astype(F32)
                + xyl[...].astype(F32))
            x_out[...] = total[:256].T.astype(BF16)
            user_out[...] = total[256:].T.astype(BF16)

        return carry

    lax.fori_loop(0, STEPS + 1, third, 0)

    def drain(k, carry):
        cc = cols(k)
        sent(zall.at[0, :, cc], Z_Y + k)
        sent(zall.at[0, :, cc], Z_E0 + k)
        sent(zall.at[0, :, cc], Z_FW + k)
        sent(gr1.at[:, :, cc], G_E1 + k)
        sent(ps.at[:, cc], M_E1 + k)
        sent(xsend.at[k], X_CORE + k)
        return carry

    lax.fori_loop(0, STEPS, drain, 0)
    sent(gr1.at[:, :, pl.ds(H, GH)], G_E1 + 8)
    sent(gr2, G_Y)
    sent(gr3, G_E0)

    @pl.when(jnp.logical_not(is_self))
    def _():
        sent(x_own, I_PERM)

    sent(place(z, c, 0, 1), I_YL)
    for i in range(2):
        sent(place(z, c, 0, 2), I_Z1 + i)
        sent(place(z, c, 0, 1), I_Z2 + i)
        sent(xz1.at[i], X_Z1 + i)
    for i in range(4):
        sent(place(z, c, 0, 2), I_CORE + i)
        sent(xz2.at[0, 0], X_Z2 + i)
    sent(xyl, X_YL)
    for s in range(7):
        sent(tsend.at[s], T_ALL + s)


def body(
    x_quant, x_scale, user_feats, scenario_ids, scenario_table, label_mask,
    saved_z, out_grad, main_weight, gate_a, gate_b,
):
    vmem = pl.BlockSpec(memory_space=pltpu.VMEM)
    hbm = pl.BlockSpec(memory_space=pl.ANY)
    outs = pl.pallas_call(
        kernel,
        out_shape=(
            jax.ShapeDtypeStruct((512, H), BF16),
            jax.ShapeDtypeStruct((64, GH), BF16),
            jax.ShapeDtypeStruct((64, H), BF16),
            jax.ShapeDtypeStruct((ROWS, 256), BF16),
            jax.ShapeDtypeStruct((ROWS, 32), BF16),
            jax.ShapeDtypeStruct((32, 128), F32),
        ),
        in_specs=[vmem] * 9 + [hbm] * 3,
        out_specs=(vmem,) * 6,
        scratch_shapes=[
            pltpu.VMEM((ROWS, H), BF16),
            pltpu.VMEM((ROWS, H), BF16),
            pltpu.VMEM((2, 512, H), BF16),
            pltpu.VMEM((4, ROWS, H), BF16),
            pltpu.VMEM((ROWS, GH), BF16),
            pltpu.VMEM((2, ROWS, GH), BF16),
            pltpu.VMEM((ROWS, GH), F32),
            pltpu.VMEM((512, ROWS), F32),
            pltpu.VMEM((2, 2, 256, 4 * ROWS), BF16),
            pltpu.VMEM((256, ROWS), BF16),
            pltpu.VMEM((2, 2, 128, H + GH), BF16),
            pltpu.VMEM((2, 128, H + GH), BF16),
            pltpu.VMEM((128, H + GH), BF16),
            pltpu.VMEM((64, H + GH), BF16),
            pltpu.VMEM((8, XB, ROWS), BF16),
            pltpu.VMEM((8, XB, ROWS), BF16),
            pltpu.VMEM((8, XB, ROWS), BF16),
            pltpu.VMEM((2, XB, ROWS), BF16),
            pltpu.VMEM((2, 2, XB, ROWS), BF16),
            pltpu.VMEM((XB, ROWS), BF16),
            pltpu.VMEM((XB, ROWS), BF16),
            pltpu.VMEM((512, H), BF16),
            pltpu.VMEM((512, H), BF16),
            pltpu.VMEM((7, 32, 128), F32),
            pltpu.VMEM((7, 32, 128), F32),
            pltpu.SemaphoreType.DMA((5,)),
            pltpu.SemaphoreType.DMA((N_SEM,)),
            pltpu.SemaphoreType.DMA((N_SEM,)),
        ],
        compiler_params=pltpu.CompilerParams(
            collective_id=0, has_side_effects=True, vmem_limit_bytes=60 * 1024 * 1024),
        cost_estimate=pl.CostEstimate(flops=21_000_000_000, bytes_accessed=28_000_000, transcendentals=1_000_000),
    )(
        x_quant, x_scale, user_feats, scenario_ids[:, None], scenario_ids[None, :], scenario_table,
        label_mask, gate_a[0], gate_b[0], saved_z[0], out_grad[0], main_weight[0],
    )
    main, grad_a, grad_b, x_grad, user, table_grad = outs
    return main[None], grad_a[None], grad_b[None], x_grad, user[:, :USER], table_grad


def solution(mesh):
    placed = (
        P("batch", "task"),
        P("batch", "task"),
        P("batch", None),
        P("batch"),
        P(),
        P("batch", "task"),
        P("task", "batch", None),
        P("task", "batch", None),
        P("task", None, None),
        P("task", None, None),
        P("task", None, None),
    )
    return jax.shard_map(
        body,
        mesh=mesh,
        in_specs=placed,
        out_specs=(
            P("task", "batch", None),
            P("task", "batch", None),
            P("task", "batch", None),
            P("batch", "task"),
            P("batch", "task"),
            P(),
        ),
        check_vma=False,
    )
```

time: 546 us -> 173 us (0.32)
  waiting for transfers between devices: 371 us -> 0 us
  Pallas kernels: 0 us -> 159 us
  blocking collectives: 86.2 us -> 0 us
  matrix products: 64.1 us -> 0 us
  between operations: 14.2 us -> 0.65 us
    reduce_scatter x4 -> x0, waiting for transfers between devices: 370 us -> none  [the longest x1 197 us: body(): lax.psum_scatter(jnp.einsum('rd,rh->dh', inputs, z_grad, preferred_elemen...]
    pallas_call x0 -> x1, Pallas kernels: none -> 159 us  [body(): pl.pallas_call(kernel, out_shape=(jax.ShapeDtypeStruct((512, H), BF16), j...]
    psum x1 -> x0, blocking collectives: 66.2 us -> none  [body(): table_grad = lax.psum(table_local, ('batch', 'task'))]
    dot_general x10 -> x0, matrix products: 64.1 us -> none  [the longest x1 32 us: body(): jnp.einsum('rd,rh->dh', inputs, z_grad, preferred_element_type=jnp.float32)]
    all_gather x1 -> x0, blocking collectives: 20 us -> none  [body(): lax.all_gather(x_scale, 'task', axis=1, tiled=True)]
    unnamed x19 -> x16, local copies, waits for them, and re-layouts: 2.54 us -> 10.5 us
    mul x1 -> x0, local copies, waits for them, and re-layouts: 5.76 us -> none  [dequantize(): values.astype(jnp.float32).reshape(row_count, blocks, width // blocks)]
  transfers between devices with their start and end apart: 6 -> 0, of which waited for: 4 -> 0; matrix products, arithmetic and copies ran while one was open for 13% -> 0% of each run, Pallas kernels for 0% -> 0%
where the time goes in v1:
time: 173 us; the launch traced here: 171 us
  Pallas kernels  159 us (92%)
  local copies, waits for them, and re-layouts  12 us (7%)
    pallas_call x1, Pallas kernels, body(): pl.pallas_call(kernel, out_shape=(jax.ShapeDtypeStruct((512, H), BF16), j...  159 us
    unnamed x16, local copies, waits for them, and re-layouts  10.5 us

profile of v1, /device:TPU:8, one launch (start us, length us, event | category | flops | bytes accessed | tf_op | source)
XLA Modules:
  0.0 171.2 jit_solution(1452105104605210289)
XLA Ops:
  0.6 1.5 copy.20.xs
  2.1 1.5 copy.22.mask_col
  3.7 1.5 copy.21.ids_col
  5.2 158.5 %shard_map.154 = (bf16[512,2048]{1,0:T(8,128)(2,1)}, bf16[64,512]{1,0:T(8,128)(2,1)}, bf16[64,2048]{1,0:T(8,128)(2,1)}, bf16[512,256]{1,0:T(8,128)(2,1)}, bf16[512,32]{1,0:T(8,128)(2,1)}, /*index=5*/f32[32,128]{1,0:T(8,128)}) custom-call(bf16[512,256]{1,0:T(8,128)(2,1)} %xq.1, bf16[512,2]{1,0:T(8,128)(2,1)} %copy.20.xs, bf16[512,384]{1,0:T(8,128)(2,1)} %feats.1, ...), custom_call_target="tpu_custom_call" | custom-call | flops 20999999488 | bytes 28000000 | tf_op jit(solution)/shard_map/pallas_call | solution.py:386
  163.7 1.6 copy.23
  165.3 0.0 copy-start.2
  165.3 0.0 copy-start.1
  165.3 0.0 copy-start
  165.3 0.0 copy-start.3
  165.3 3.2 %copy.29 = bf16[1,512,2048]{2,1,0:T(8,128)(2,1)} copy(bf16[1,512,2048]{2,1,0:T(8,128)(2,1)} %bitcast.11) | data formatting | bytes 4194304
  168.5 0.0 copy-done.2
  168.5 0.6 copy.30
  169.2 0.0 copy-done.1
  169.2 0.7 copy.31
  169.9 0.0 copy-done
  169.9 0.7 copy.32
  170.6 0.0 copy-done.3
  170.6 0.6 copy.33
Async XLA Ops:
  165.3 3.2 %copy-start.2 = (bf16[64,512]{1,0:T(8,128)(2,1)S(1)}, bf16[64,512]{1,0:T(8,128)(2,1)}, u32[]{:S(2)}) copy-start(bf16[64,512]{1,0:T(8,128)(2,1)} %get-tuple-element.13) | copy-start | bytes 196612
  165.3 3.9 %copy-start.1 = (bf16[64,2048]{1,0:T(8,128)(2,1)S(1)}, bf16[64,2048]{1,0:T(8,128)(2,1)}, u32[]{:S(2)}) copy-start(bf16[64,2048]{1,0:T(8,128)(2,1)} %get-tuple-element.14) | copy-start | bytes 786436
  165.3 4.6 %copy-start = (bf16[512,256]{1,0:T(8,128)(2,1)S(1)}, bf16[512,256]{1,0:T(8,128)(2,1)}, u32[]{:S(2)}) copy-start(bf16[512,256]{1,0:T(8,128)(2,1)} %get-tuple-element.39) | copy-start | bytes 786436
  165.3 5.3 %copy-start.3 = (f32[32,128]{1,0:T(8,128)S(1)}, f32[32,128]{1,0:T(8,128)}, u32[]{:S(2)}) copy-start(f32[32,128]{1,0:T(8,128)} %get-tuple-element.41) | copy-start | bytes 49156

commit v2 on v1

v2 whole, which is shorter than its diff:
```python
import jax
import jax.numpy as jnp
from jax import lax
from jax.experimental import pallas as pl
from jax.experimental.pallas import tpu as pltpu
from jax.sharding import PartitionSpec as P

MESH = pl.DeviceIdType.MESH
F32 = jnp.float32
BF16 = jnp.bfloat16

ROWS = 512
H = 2048
GH = 512
UD = 384
CH = 256
STEPS = H // CH
XB = 288
USER = 24
CAP = 320
DEPTH = 4 * CAP
LAG = 3

Z_Y, Z_E0, Z_FW = 0, 8, 16
G_E1, G_Y, G_E0 = 24, 33, 34
I_PERM, I_YL, I_Z1, I_Z2, I_CORE = 35, 36, 37, 41, 45
M_E1 = 49
X_CORE, X_Z1, X_Z2, X_YL = 57, 65, 67, 71
T_ALL = 72
S_ALL = 79
N_SEM = 82


def nt(a, b):
    return lax.dot_general(a, b, (((1,), (1,)), ((), ())), preferred_element_type=F32)


def nn(a, b):
    return jnp.dot(a, b, preferred_element_type=F32)


def kernel(
    xq, xs, feats, ids, table, mask_in, ga, gb, sz_hbm, og_hbm, w_hbm,
    main_out, ga_out, gb_out, x_out, user_out, table_out, flag_out,
    sz, og, wbuf, zfull, zc, gin_in, act, a_back, gint, aall, ac, x_own, pick, sel,
    gpart, gr1, gr2, gr3, xsend, xkeep, xcore, xz1, xz2, xylsend, xyl, ps, pr, tsend, trecv,
    lsem, ssem, rsem,
):
    bi = lax.axis_index("batch")
    ti = lax.axis_index("task")
    yh, x = bi // 4, bi % 4
    yl, z, c = ti // 8, (ti // 2) % 4, ti % 2
    x0 = x + 1 - 2 * (x % 2)
    x1 = 3 - x
    xp = x // 2
    z0 = z + 1 - 2 * (z % 2)

    def dev(yh_, x_, yl_, z_, c_):
        return (yh_ * 4 + x_, yl_ * 8 + z_ * 2 + c_)

    d_y = dev(1 - yh, x, yl, z, c)
    d_e0 = dev(yh, x0, yl, z, c)
    d_e1 = dev(yh, x1, yl, z, c)
    d_c = dev(yh, x, yl, z, 1 - c)
    d_yl = dev(yh, x, 1 - yl, z, c)
    d_zp = dev(yh, x, yl, (z + 1) % 4, c)
    d_zm = dev(yh, x, yl, (z + 3) % 4, c)
    member = jnp.logical_or(z == x, z == 3 - x)
    ksel = jnp.where(member, 0, 1)
    is_self = jnp.logical_and(member, yh == yl)
    d_diag = dev(1 - yh, x0, yl, z, c)
    d_perm = dev(yl, x + ksel * (x0 - x), yh, z + ksel * (z0 - z), c)

    def rcopy(src, dst, i, target):
        return pltpu.make_async_remote_copy(
            src_ref=src, dst_ref=dst, send_sem=ssem.at[i], recv_sem=rsem.at[i],
            device_id=target, device_id_type=MESH)

    def send(src, dst, i, target):
        rcopy(src, dst, i, target).start()

    def got(ref, i):
        rcopy(ref, ref, i, d_c).wait_recv()

    def sent(ref, i):
        rcopy(ref, ref, i, d_c).wait_send()

    def packed(s):
        return pl.ds(pl.multiple_of(s * CAP, CAP), CAP)

    def cols(k):
        return pl.ds(pl.multiple_of(k * CH, CH), CH)

    def wcopy(k):
        return pltpu.make_async_copy(
            w_hbm.at[pl.ds(pl.multiple_of(k * 512, 512), 512)], wbuf.at[k % 2], lsem.at[2 + k % 2])

    sz_copy = pltpu.make_async_copy(sz_hbm, sz, lsem.at[0])
    og_copy = pltpu.make_async_copy(og_hbm, og, lsem.at[1])
    sz_copy.start()
    og_copy.start()
    wcopy(0).start()
    wcopy(1).start()

    barrier = pltpu.get_barrier_semaphore()
    for target in (d_y, d_e0, d_e1, d_c, d_yl, d_zp, d_zm, d_diag):
        pl.semaphore_signal(barrier, inc=1, device_id=target, device_id_type=MESH)

    @pl.when(jnp.logical_not(is_self))
    def _():
        pl.semaphore_signal(barrier, inc=1, device_id=d_perm, device_id_type=MESH)

    half = xq.shape[1] // 2
    for j in range(2):
        part = xq[:, j * half:(j + 1) * half].astype(F32).T * xs[j:j + 1, :].astype(F32)
        x_own[j * half:(j + 1) * half, :] = part.astype(BF16)

    mask_row = jnp.broadcast_to(mask_in[...], (8, ROWS)).astype(F32)
    before = (
        lax.broadcasted_iota(jnp.int32, (ROWS, ROWS), 0) < lax.broadcasted_iota(jnp.int32, (ROWS, ROWS), 1)
    ).astype(BF16)
    rank = nn(mask_row.astype(BF16), before)
    sel[yh] = jnp.where(mask_row > 0, rank, -1.0)

    def picker(s):
        return (
            lax.broadcasted_iota(jnp.int32, (CAP, ROWS), 0).astype(F32) == sel[s, 0:1, :]
        ).astype(BF16)

    pick[...] = picker(yh)

    pl.semaphore_wait(barrier, jnp.where(is_self, 8, 9))

    def place(zz, core, first, count):
        d_ = jnp.where(zz // 2 == xp, 1, 0)
        k_ = jnp.where(jnp.logical_or(zz == x, zz == 3 - x), 0, 1)
        off = pl.multiple_of((k_ * 2 + first) * ROWS, ROWS)
        return aall.at[d_, core, :, pl.ds(off, count * ROWS)]

    @pl.when(is_self)
    def _():
        local = pltpu.make_async_copy(x_own, place(z, c, yl, 1), lsem.at[4])
        local.start()
        local.wait()

    @pl.when(jnp.logical_not(is_self))
    def _():
        send(x_own, place(z, c, yh, 1), I_PERM, d_perm)

    send(sel.at[yh], sel.at[yh], S_ALL, d_y)
    send(sel.at[yh], sel.at[2 + yh], S_ALL + 1, d_e0)
    send(sel.at[yh], sel.at[2 + yh], S_ALL + 2, d_diag)

    onehot_t = (ids[...] == lax.broadcasted_iota(jnp.int32, (32, ROWS), 0)).astype(F32)
    gin_in[:, :UD] = feats[...]
    gin_in[:, UD:] = nn(onehot_t.T.astype(BF16), table[...]).astype(BF16)
    a_pre = nn(gin_in[...], ga[...])
    a_act = jnp.maximum(a_pre, 0.0)
    act[0] = a_act.astype(BF16)
    act[1] = a_act.T.astype(BF16)
    a_back[...] = jnp.zeros_like(a_back)
    mask = mask_row.T[:, 0:1]
    sz_copy.wait()
    og_copy.wait()

    def first(k, carry):
        cc = cols(k)
        gate = 2.0 * jax.nn.sigmoid(nn(act[0], gb[:, cc]))
        masked = og[:, cc].astype(F32) * mask
        pre = sz[:, cc].astype(F32)
        mg = masked * gate
        zk = jnp.where(pre > 0, mg, 0.0).astype(BF16)
        zfull[:, cc] = zk
        zc[packed(yh), cc] = nn(pick[...], zk).astype(BF16)

        @pl.when(k < 4)
        def _():
            send(zc.at[packed(yh), cc], zc.at[packed(2 + yh), cc], Z_E0 + k, d_e0)

        @pl.when(k == 5)
        def _():
            @pl.when(jnp.logical_not(is_self))
            def _():
                got(place(z, c, yl, 1), I_PERM)

            mine = place(z, c, yl, 1)
            send(mine, mine, I_YL, d_yl)
            send(mine, mine, I_Z1, d_zp)
            send(mine, mine, I_Z1 + 1, d_zm)

            def early(n, carry):
                send(zc.at[packed(yh), cols(n)], zc.at[packed(yh), cols(n)], Z_Y + n, d_y)
                return carry

            lax.fori_loop(0, 5, early, 0)

        @pl.when(k >= 5)
        def _():
            send(zc.at[packed(yh), cc], zc.at[packed(yh), cc], Z_Y + k, d_y)

        u = (jnp.maximum(pre, 0.0) * mg * (1.0 - 0.5 * gate)).astype(BF16)
        part = nn(act[1], u).astype(BF16)
        for i in range(2):
            for j in range(2):
                r = (i * 2 + j) * 128
                gpart[i, j, :, cc] = part[r:r + 128]
        send(gpart.at[:, 1 - xp, :, cc], gr1.at[:, :, cc], G_E1 + k, d_e1)
        a_back[...] += nt(u, gb[:, cc])
        return carry

    lax.fori_loop(0, STEPS, first, 0)

    a_grad = jnp.where(act[0].astype(F32) > 0, a_back[...], 0.0).astype(BF16)
    part = nn(gin_in[...].astype(F32).T.astype(BF16), a_grad).astype(BF16)
    for i in range(2):
        for j in range(2):
            r = (i * 2 + j) * 128
            gpart[i, j, :, H:] = part[r:r + 128]
    send(gpart.at[:, 1 - xp, :, pl.ds(H, GH)], gr1.at[:, :, pl.ds(H, GH)], G_E1 + 8, d_e1)
    gint[...] = nt(ga[...], a_grad)
    scen = nt(a_grad, ga[UD:, :])
    tsend[0, :32] = lax.dot_general(
        onehot_t, scen, (((1,), (0,)), ((), ())), precision=lax.Precision.HIGHEST, preferred_element_type=F32)
    over = jnp.maximum(jnp.sum(mask_row, axis=1, keepdims=True) - CAP, 0.0)
    tsend[0, 32:] = jnp.broadcast_to(over, (8, 128))
    t_partners = (d_c, dev(yh, x, yl, z0, c), dev(yh, x, yl, 3 - z, c), d_yl, d_y, d_e1, d_e0)
    send(tsend.at[0], trecv.at[0], T_ALL, t_partners[0])

    def user_rows(t):
        rows = gint[pl.ds(pl.multiple_of(t * USER, 8), USER), :]
        return jnp.concatenate([rows, jnp.zeros((XB - 256 - USER, ROWS), F32)], axis=0).astype(BF16)

    zn, zb, zf = (z + 1) % 4, (z + 3) % 4, (z + 2) % 4

    def half_rows(zz, first, h):
        d_ = jnp.where(zz // 2 == xp, 1, 0)
        k_ = jnp.where(jnp.logical_or(zz == x, zz == 3 - x), 0, 1)
        off = pl.multiple_of((k_ * 2 + first) * ROWS, ROWS)
        return aall.at[d_, c, pl.ds(h * 128, 128), pl.ds(off, ROWS)]

    def z_forward(n, first):
        got(place(zb, c, first, 1), I_Z1 + 2 * n)
        got(place(zn, c, first, 1), I_Z1 + 2 * n + 1)
        low, high = half_rows(zb, first, 0), half_rows(zn, first, 1)
        send(low, low, I_Z2 + 2 * n, d_zp)
        send(high, high, I_Z2 + 2 * n + 1, d_zm)

    def to_core(zz, i):
        mine = place(zz, c, 0, 2)
        send(mine, mine, I_CORE + i, d_c)

    def x_block(k, carry):
        wcopy(k).wait()
        wrows = wbuf.at[k % 2]
        other = 1 - c
        xsend[k, :256, :] = nt(wrows[pl.ds(pl.multiple_of(other * 256, 256), 256), :], zfull[...]).astype(BF16)
        xsend[k, 256:, :] = user_rows(k * 2 + other)
        send(xsend.at[k], xcore.at[k], X_CORE + k, d_c)
        xkeep[k, :256, :] = nt(wrows[pl.ds(pl.multiple_of(c * 256, 256), 256), :], zfull[...]).astype(BF16)
        xkeep[k, 256:, :] = user_rows(k * 2 + c)

        @pl.when(k < STEPS - 2)
        def _():
            wcopy(k + 2).start()

        return carry

    def second(k):
        cc = cols(k)

        @pl.when(k < 4)
        def _():
            lax.fori_loop(2 * k, 2 * k + 2, x_block, 0)

        @pl.when(k == 0)
        def _():
            got(place(z, c, 1 - yl, 1), I_YL)
            mine = place(z, c, 1 - yl, 1)
            send(mine, mine, I_Z1 + 2, d_zp)
            send(mine, mine, I_Z1 + 3, d_zm)
            to_core(z, 0)
            z_forward(0, yl)

        @pl.when(k == 1)
        def _():
            z_forward(1, 1 - yl)
            to_core(zb, 1)
            to_core(zn, 2)

        @pl.when(k == 2)
        def _():
            for n, first in enumerate((yl, 1 - yl)):
                got(half_rows(zf, first, 0), I_Z2 + 2 * n)
                got(half_rows(zf, first, 1), I_Z2 + 2 * n + 1)
            to_core(zf, 3)

        got(zc.at[packed(1 - yh), cc], Z_Y + k)
        send(zc.at[packed(1 - yh), cc], zc.at[packed(3 - yh), cc], Z_FW + k, d_e0)

        @pl.when(k < 4)
        def _():
            more = cols(k + 4)
            send(zc.at[packed(yh), more], zc.at[packed(2 + yh), more], Z_E0 + 4 + k, d_e0)

    def table_step(s):
        got(trecv.at[s - 1], T_ALL + s - 1)
        tsend[s] = tsend[s - 1] + trecv[s - 1]
        send(tsend.at[s], trecv.at[s], T_ALL + s, t_partners[s])

    def pack_inputs():
        for i, zz in enumerate((z, zb, zn, zf)):
            got(place(zz, 1 - c, 0, 2), I_CORE + i)
        got(sel.at[1 - yh], S_ALL)
        got(sel.at[2 + yh], S_ALL + 1)
        got(sel.at[3 - yh], S_ALL + 2)
        for s in range(4):
            p = picker(s)
            for d_ in range(2):
                for j in range(2):
                    ac[d_, j, :, s * CAP:(s + 1) * CAP] = nt(
                        aall[d_, j, :, s * ROWS:(s + 1) * ROWS], p).astype(BF16)

    def core_sum():
        def one(n, carry):
            got(xcore.at[n], X_CORE + n)
            xkeep[n] = (xkeep[n].astype(F32) + xcore[n].astype(F32)).astype(BF16)
            return carry

        lax.fori_loop(0, STEPS, one, 0)
        send(xkeep.at[zf], xz1.at[0], X_Z1, d_zp)
        send(xkeep.at[4 + zf], xz1.at[1], X_Z1 + 1, d_zm)

    def gate_e1():
        for n in range(STEPS):
            got(gr1.at[:, :, pl.ds(n * CH, CH)], G_E1 + n)
        got(gr1.at[:, :, pl.ds(H, GH)], G_E1 + 8)
        gpart[1 - yh, xp] = (gpart[1 - yh, xp].astype(F32) + gr1[1 - yh].astype(F32)).astype(BF16)
        send(gpart.at[1 - yh, xp], gr2, G_Y, d_y)

    def gate_y():
        got(gr2, G_Y)
        gpart[yh, xp] = (
            gpart[yh, xp].astype(F32) + gr1[yh].astype(F32) + gr2[...].astype(F32)).astype(BF16)
        far = pl.ds(pl.multiple_of((x0 % 2) * 64, 64), 64)
        send(gpart.at[yh, xp, far], gr3, G_E0, d_e0)

    def gate_e0():
        got(gr3, G_E0)
        near = pl.ds(pl.multiple_of((x % 2) * 64, 64), 64)
        total = gpart[yh, xp, near, :].astype(F32) + gr3[...].astype(F32)
        gb_out[...] = total[:, :H].astype(BF16)
        ga_out[...] = total[:, H:].astype(BF16)

    def x_z1():
        got(xz1.at[0], X_Z1)
        got(xz1.at[1], X_Z1 + 1)
        xkeep[zn] = (xkeep[zn].astype(F32) + xz1[0].astype(F32)).astype(BF16)
        xkeep[4 + zb] = (xkeep[4 + zb].astype(F32) + xz1[1].astype(F32)).astype(BF16)
        for h in range(2):
            send(xkeep.at[h * 4 + zn], xz2.at[0, h], X_Z2 + 2 * h, d_zp)
            send(xkeep.at[h * 4 + zb], xz2.at[1, h], X_Z2 + 1 + 2 * h, d_zm)

    def x_z2():
        for h in range(2):
            got(xz2.at[0, h], X_Z2 + 2 * h)
            got(xz2.at[1, h], X_Z2 + 1 + 2 * h)
        xylsend[...] = (
            xkeep[(1 - yl) * 4 + z].astype(F32) + xz2[0, 1 - yl].astype(F32) + xz2[1, 1 - yl].astype(F32)
        ).astype(BF16)
        send(xylsend, xyl, X_YL, d_yl)

    def x_last():
        got(xyl, X_YL)
        total = (
            xkeep[yl * 4 + z].astype(F32) + xz2[0, yl].astype(F32) + xz2[1, yl].astype(F32)
            + xyl[...].astype(F32))
        x_out[...] = total[:256].T.astype(BF16)
        user_out[...] = total[256:256 + USER].astype(BF16)

    def table_last():
        got(trecv.at[6], T_ALL + 6)
        total = tsend[6] + trecv[6]
        table_out[...] = total[:32]
        flag_out[0, 0] = total[32, 0]

    def table_at(s):
        return lambda: table_step(s)

    extra = {
        1: (table_at(1),),
        3: (table_at(2),),
        4: (core_sum,),
        5: (table_at(3), x_z1, gate_e1),
        7: (table_at(4),),
        8: (table_at(5), x_z2),
        9: (table_at(6), gate_y),
        10: (x_last,),
        11: (table_last, gate_e0),
    }

    def step(i, carry):
        @pl.when(i < STEPS)
        def _():
            second(i)

        @pl.when(i == LAG)
        def _():
            pack_inputs()

        j = i - LAG

        @pl.when(jnp.logical_and(j >= 0, j < STEPS))
        def _():
            cc = cols(j)
            got(zc.at[packed(2 + yh), cc], Z_E0 + j)
            got(zc.at[packed(3 - yh), cc], Z_FW + j)
            for h in range(2):
                ps[h * 256:(h + 1) * 256, cc] = nn(ac[0, h], zc[:, cc]).astype(BF16)
            send(ps.at[:, cc], pr.at[:, cc], M_E1 + j, d_e1)

        for at, calls in extra.items():

            @pl.when(i == at)
            def _():
                for call in calls:
                    call()

        @pl.when(jnp.logical_and(j >= 1, j <= STEPS))
        def _():
            cc = cols(j - 1)
            got(pr.at[:, cc], M_E1 + j - 1)
            for h in range(2):
                total = pr[h * 256:(h + 1) * 256, cc].astype(F32) + nn(ac[1, h], zc[:, cc])
                main_out[h * 256:(h + 1) * 256, cc] = total.astype(BF16)

        return carry

    lax.fori_loop(0, STEPS + LAG + 1, step, 0)

    def drain(k, carry):
        cc = cols(k)
        sent(zc.at[packed(0), cc], Z_Y + k)
        sent(zc.at[packed(0), cc], Z_E0 + k)
        sent(zc.at[packed(0), cc], Z_FW + k)
        sent(gr1.at[:, :, cc], G_E1 + k)
        sent(ps.at[:, cc], M_E1 + k)
        sent(xsend.at[k], X_CORE + k)
        return carry

    lax.fori_loop(0, STEPS, drain, 0)
    sent(gr1.at[:, :, pl.ds(H, GH)], G_E1 + 8)
    sent(gr2, G_Y)
    sent(gr3, G_E0)

    @pl.when(jnp.logical_not(is_self))
    def _():
        sent(x_own, I_PERM)

    sent(place(z, c, 0, 1), I_YL)
    for i in range(4):
        sent(place(z, c, 0, 1), I_Z1 + i)
        sent(half_rows(z, 0, 0), I_Z2 + i)
    for i in range(2):
        sent(xz1.at[i], X_Z1 + i)
    for i in range(3):
        sent(sel.at[0], S_ALL + i)
    for i in range(4):
        sent(place(z, c, 0, 2), I_CORE + i)
        sent(xz2.at[0, 0], X_Z2 + i)
    sent(xyl, X_YL)
    for s in range(7):
        sent(tsend.at[s], T_ALL + s)


def copy_kernel(*refs):
    n = len(refs) // 2
    for i in range(n):
        refs[n + i][...] = refs[i][...]


def copy_out(*arrays):
    vmem = pl.BlockSpec(memory_space=pltpu.VMEM)
    return pl.pallas_call(
        copy_kernel,
        out_shape=tuple(jax.ShapeDtypeStruct(a.shape, a.dtype) for a in arrays),
        in_specs=[vmem] * len(arrays),
        out_specs=(vmem,) * len(arrays),
    )(*arrays)


def main_grad_wide(
    x_quant, x_scale, user_feats, scenario_ids, scenario_table, label_mask, saved_z, out_grad, gate_a, gate_b,
):
    onehot = (scenario_ids[:, None] == jnp.arange(32, dtype=jnp.int32)[None, :]).astype(BF16)
    scen_rows = jnp.dot(onehot, scenario_table, preferred_element_type=F32).astype(BF16)
    gate_in = jnp.concatenate([user_feats, scen_rows], axis=1)
    a_act = jnp.maximum(jnp.dot(gate_in, gate_a[0], preferred_element_type=F32), 0.0).astype(BF16)
    gate = 2.0 * jax.nn.sigmoid(jnp.dot(a_act, gate_b[0], preferred_element_type=F32))
    masked = out_grad[0].astype(F32) * label_mask.astype(F32)
    z_grad = (masked * gate * (saved_z[0] > 0)).astype(BF16)
    blocks = x_scale.shape[1]
    own = (
        x_quant.astype(F32).reshape(ROWS, blocks, -1) * x_scale.astype(F32)[:, :, None]
    ).reshape(ROWS, -1).astype(BF16)
    inputs = lax.all_to_all(jnp.broadcast_to(own, (16, *own.shape)), "task", 0, 0)
    partial = jnp.einsum("trd,rh->tdh", inputs, z_grad, preferred_element_type=F32).astype(BF16)
    parts = lax.all_to_all(partial.reshape(8, 512, H), "batch", 0, 0)
    return jnp.sum(parts.astype(F32), axis=0).astype(BF16)


def body(
    x_quant, x_scale, user_feats, scenario_ids, scenario_table, label_mask,
    saved_z, out_grad, main_weight, gate_a, gate_b,
):
    vmem = pl.BlockSpec(memory_space=pltpu.VMEM)
    hbm = pl.BlockSpec(memory_space=pl.ANY)
    outs = pl.pallas_call(
        kernel,
        out_shape=(
            jax.ShapeDtypeStruct((512, H), BF16),
            jax.ShapeDtypeStruct((64, GH), BF16),
            jax.ShapeDtypeStruct((64, H), BF16),
            jax.ShapeDtypeStruct((ROWS, 256), BF16),
            jax.ShapeDtypeStruct((USER, ROWS), BF16),
            jax.ShapeDtypeStruct((32, 128), F32),
            jax.ShapeDtypeStruct((1, 1), F32),
        ),
        in_specs=[vmem] * 8 + [hbm] * 3,
        out_specs=(vmem,) * 6 + (pl.BlockSpec(memory_space=pltpu.SMEM),),
        scratch_shapes=[
            pltpu.VMEM((ROWS, H), BF16),
            pltpu.VMEM((ROWS, H), BF16),
            pltpu.VMEM((2, 512, H), BF16),
            pltpu.VMEM((ROWS, H), BF16),
            pltpu.VMEM((DEPTH, H), BF16),
            pltpu.VMEM((ROWS, GH), BF16),
            pltpu.VMEM((2, ROWS, GH), BF16),
            pltpu.VMEM((ROWS, GH), F32),
            pltpu.VMEM((512, ROWS), F32),
            pltpu.VMEM((2, 2, 256, 4 * ROWS), BF16),
            pltpu.VMEM((2, 2, 256, DEPTH), BF16),
            pltpu.VMEM((256, ROWS), BF16),
            pltpu.VMEM((CAP, ROWS), BF16),
            pltpu.VMEM((4, 8, ROWS), F32),
            pltpu.VMEM((2, 2, 128, H + GH), BF16),
            pltpu.VMEM((2, 128, H + GH), BF16),
            pltpu.VMEM((128, H + GH), BF16),
            pltpu.VMEM((64, H + GH), BF16),
            pltpu.VMEM((8, XB, ROWS), BF16),
            pltpu.VMEM((8, XB, ROWS), BF16),
            pltpu.VMEM((8, XB, ROWS), BF16),
            pltpu.VMEM((2, XB, ROWS), BF16),
            pltpu.VMEM((2, 2, XB, ROWS), BF16),
            pltpu.VMEM((XB, ROWS), BF16),
            pltpu.VMEM((XB, ROWS), BF16),
            pltpu.VMEM((512, H), BF16),
            pltpu.VMEM((512, H), BF16),
            pltpu.VMEM((7, 40, 128), F32),
            pltpu.VMEM((7, 40, 128), F32),
            pltpu.SemaphoreType.DMA((5,)),
            pltpu.SemaphoreType.DMA((N_SEM,)),
            pltpu.SemaphoreType.DMA((N_SEM,)),
        ],
        compiler_params=pltpu.CompilerParams(
            collective_id=0, has_side_effects=True, vmem_limit_bytes=60 * 1024 * 1024),
        cost_estimate=pl.CostEstimate(flops=21_000_000_000, bytes_accessed=28_000_000, transcendentals=1_000_000),
    )(
        x_quant, x_scale.T, user_feats, scenario_ids[None, :], scenario_table,
        label_mask.T, gate_a[0], gate_b[0], saved_z[0], out_grad[0], main_weight[0],
    )
    main, grad_a, grad_b, x_grad, user, table_grad = copy_out(*outs[:6])
    args = (
        x_quant, x_scale, user_feats, scenario_ids, scenario_table, label_mask, saved_z, out_grad, gate_a, gate_b)
    _, main = lax.while_loop(
        lambda carry: carry[0] > 0,
        lambda carry: (jnp.zeros_like(carry[0]), main_grad_wide(*args)),
        (outs[6][0, 0], main))
    return main[None], grad_a[None], grad_b[None], x_grad, user.T, table_grad


def solution(mesh):
    placed = (
        P("batch", "task"),
        P("batch", "task"),
        P("batch", None),
        P("batch"),
        P(),
        P("batch", "task"),
        P("task", "batch", None),
        P("task", "batch", None),
        P("task", None, None),
        P("task", None, None),
        P("task", None, None),
    )
    return jax.shard_map(
        body,
        mesh=mesh,
        in_specs=placed,
        out_specs=(
            P("task", "batch", None),
            P("task", "batch", None),
            P("task", "batch", None),
            P("batch", "task"),
            P("batch", "task"),
            P(),
        ),
        check_vma=False,
    )
```

time: 173 us -> 105 us (0.61)
  Pallas kernels: 159 us -> 103 us
  local copies, waits for them, and re-layouts: 12 us -> 0.17 us
    pallas_call x1, Pallas kernels: 159 us -> 99.5 us  [body(): pl.pallas_call(kernel, out_shape=(jax.ShapeDtypeStruct((512, H), BF16), j...]
    unnamed x16 -> x14, local copies, waits for them, and re-layouts: 10.5 us -> 0.03 us
    pallas_call x0 -> x1, Pallas kernels: none -> 3.29 us  [copy_out(): pl.pallas_call(copy_kernel, out_shape=tuple((jax.ShapeDtypeStruct(a.shape...]
where the time goes in v2:
time: 105 us
  Pallas kernels  103 us (98%)
    pallas_call x1, Pallas kernels, body(): pl.pallas_call(kernel, out_shape=(jax.ShapeDtypeStruct((512, H), BF16), j...  99.5 us
    pallas_call x1, Pallas kernels, copy_out(): pl.pallas_call(copy_kernel, out_shape=tuple((jax.ShapeDtypeStruct(a.shape...  3.29 us

profile of v2, /device:TPU:8, one launch (start us, length us, event | category | flops | bytes accessed | tf_op | source)
XLA Modules:
  0.0 104.6 jit_solution(7323895742743724636)
XLA Ops:
  0.6 0.0 copy-start
  0.6 0.0 copy-start.1
  0.7 0.0 copy-start.2
  0.7 0.0 copy-start.3
  0.7 0.0 copy-start.4
  0.7 0.0 copy-start.5
  0.7 0.0 copy-start.6
  0.7 99.5 %shard_map.154 = (bf16[512,2048]{1,0:T(8,128)(2,1)}, bf16[64,512]{1,0:T(8,128)(2,1)}, bf16[64,2048]{1,0:T(8,128)(2,1)}, bf16[512,256]{1,0:T(8,128)(2,1)}, bf16[2...) custom-call(bf16[512,256]{1,0:T(8,128)(2,1)} %xq.1, bf16[2,512]{1,0:T(2,128)(2,1)} %bitcast.47, ...), custom_call_target="tpu_custom_call" | custom-call | flops 20999999488 | bytes 28000000 | tf_op jit(solution)/shard_map/pallas_call | solution.py:517
  100.2 3.3 %shard_map.155 = (bf16[512,2048]{1,0:T(8,128)(2,1)}, bf16[64,512]{1,0:T(8,128)(2,1)}, bf16[64,2048]{1,0:T(8,128)(2,1)}, bf16[512,256]{1,0:T(8,128)(2,1)}, bf16[24,512]{1,0:T(8,128)(2,1)}, /*index=5*/f32[32,128]{1,0:T(8,128)}) custom-call(bf16[512,2048]{1,0:T(8,128)(2,1)} %get-tuple-element.80.refs_0_, bf16[64,512]{1,0:T(8,128)(2,1)} %get-tuple-element.81.refs_1_, ...), custom_call_target="tpu_custom_call" | custom-call | tf_op jit(solution)/shard_map/pallas_call | solution.py:483
  103.5 0.0 copy-done
  103.5 0.1 copy.17
  103.7 0.0 copy-done.1
  103.7 0.0 copy-done.2
  103.7 0.0 copy-done.3
  103.7 0.0 copy-done.4
  103.7 0.0 copy-done.5
  103.7 0.0 copy-done.6
  103.7 0.8 while.9
Async XLA Ops:
  0.6 102.9 %copy-start = (bf16[512,256]{1,0:T(8,128)(2,1)S(1)}, bf16[512,256]{1,0:T(8,128)(2,1)}, u32[]{:S(2)}) copy-start(bf16[512,256]{1,0:T(8,128)(2,1)} %xq.1) | copy-start | bytes 786436
  0.6 103.0 %copy-start.1 = (bf16[32,128]{1,0:T(8,128)(2,1)S(1)}, bf16[32,128]{1,0:T(8,128)(2,1)}, u32[]{:S(2)}) copy-start(bf16[32,128]{1,0:T(8,128)(2,1)} %table.1) | copy-start | bytes 24580
  0.7 103.0 %copy-start.2 = (s32[512]{0:T(512)S(1)}, s32[512]{0:T(512)}, u32[]{:S(2)}) copy-start(s32[512]{0:T(512)} %param.16) | copy-start | bytes 6148
  0.7 103.0 %copy-start.3 = (bf16[512,2]{0,1:T(2,128)(2,1)S(1)}, bf16[512,2]{0,1:T(2,128)(2,1)}, u32[]{:S(2)}) copy-start(bf16[512,2]{0,1:T(2,128)(2,1)} %param.14) | copy-start | bytes 6148
  0.7 103.0 %copy-start.4 = (s32[512,1]{0,1:T(1,128)S(1)}, s32[512,1]{0,1:T(1,128)}, u32[]{:S(2)}) copy-start(s32[512,1]{0,1:T(1,128)} %param.18) | copy-start | bytes 6148
  0.7 103.0 %copy-start.5 = (bf16[1,512,2048]{2,1,0:T(8,128)(2,1)S(1)}, bf16[1,512,2048]{2,1,0:T(8,128)(2,1)}, u32[]{:S(2)}) copy-start(bf16[1,512,2048]{2,1,0:T(8,128)(2,1)} %param.23) | copy-start | bytes 6291460
  0.7 103.0 %copy-start.6 = (bf16[1,512,512]{2,1,0:T(8,128)(2,1)S(1)}, bf16[1,512,512]{2,1,0:T(8,128)(2,1)}, u32[]{:S(2)}) copy-start(bf16[1,512,512]{2,1,0:T(8,128)(2,1)} %param.22) | copy-start | bytes 1572868

commit v3 on v2

--- a/solution.py
+++ b/solution.py
@@ -1,3 +1,5 @@
+import functools
+
 import jax
 import jax.numpy as jnp
 from jax import lax
@@ -19,16 +21,19 @@
 USER = 24
 CAP = 320
 DEPTH = 4 * CAP
-LAG = 3
+FIRST = 6
+AHEAD = 2
+LAG = 2
 
 Z_Y, Z_E0, Z_FW = 0, 8, 16
 G_E1, G_Y, G_E0 = 24, 33, 34
-I_PERM, I_YL, I_Z1, I_Z2, I_CORE = 35, 36, 37, 41, 45
-M_E1 = 49
-X_CORE, X_Z1, X_Z2, X_YL = 57, 65, 67, 71
-T_ALL = 72
-S_ALL = 79
-N_SEM = 82
+I_PERM, I_YL, I_Z1, I_Z2, I_CORE = 35, 37, 39, 47, 51
+M_E1 = 55
+X_CORE, X_Z1, X_Z2, X_YL = 63, 71, 73, 77
+T_ALL = 78
+S_ALL = 85
+I_WAY = 88
+N_SEM = 90
 
 
 def nt(a, b):
@@ -40,10 +45,10 @@
 
 
 def kernel(
-    xq, xs, feats, ids, table, mask_in, ga, gb, sz_hbm, og_hbm, w_hbm,
+    xs, ids, table, mask_in, xq_hbm, feats_hbm, ga_hbm, gb_hbm, sz_hbm, og_hbm, w_hbm,
     main_out, ga_out, gb_out, x_out, user_out, table_out, flag_out,
-    sz, og, wbuf, zfull, zc, gin_in, act, a_back, gint, aall, ac, x_own, pick, sel,
-    gpart, gr1, gr2, gr3, xsend, xkeep, xcore, xz1, xz2, xylsend, xyl, ps, pr, tsend, trecv,
+    xq, feats, ga, gb, sz, og, wbuf, zfull, zc, gin_in, act, a_back, gint, aall, ac, x_own, x_way, pick, sel,
+    gpart, gr1, gr2, gr3, xsend, xkeep, xcore, xz1, xz2, xylsend, xyl, ps, pr, main_v, tsend, trecv,
     lsem, ssem, rsem,
 ):
     bi = lax.axis_index("batch")
@@ -66,10 +71,11 @@
     d_zp = dev(yh, x, yl, (z + 1) % 4, c)
     d_zm = dev(yh, x, yl, (z + 3) % 4, c)
     member = jnp.logical_or(z == x, z == 3 - x)
-    ksel = jnp.where(member, 0, 1)
-    is_self = jnp.logical_and(member, yh == yl)
+    moved = jnp.logical_not(member)
+    turn = yh != yl
     d_diag = dev(1 - yh, x0, yl, z, c)
-    d_perm = dev(yl, x + ksel * (x0 - x), yh, z + ksel * (z0 - z), c)
+    d_xz = dev(yh, x0, yl, z0, c)
+    d_turn = dev(yl, x, yh, z, c)
 
     def rcopy(src, dst, i, target):
         return pltpu.make_async_remote_copy(
@@ -95,10 +101,12 @@
         return pltpu.make_async_copy(
             w_hbm.at[pl.ds(pl.multiple_of(k * 512, 512), 512)], wbuf.at[k % 2], lsem.at[2 + k % 2])
 
-    sz_copy = pltpu.make_async_copy(sz_hbm, sz, lsem.at[0])
-    og_copy = pltpu.make_async_copy(og_hbm, og, lsem.at[1])
-    sz_copy.start()
-    og_copy.start()
+    loads = [
+        pltpu.make_async_copy(src, dst, lsem.at[i]) for i, src, dst in (
+            (5, xq_hbm, xq), (6, feats_hbm, feats), (7, ga_hbm, ga), (8, gb_hbm, gb), (0, sz_hbm, sz), (1, og_hbm, og))
+    ]
+    for load in loads:
+        load.start()
     wcopy(0).start()
     wcopy(1).start()
 
@@ -106,10 +114,15 @@
     for target in (d_y, d_e0, d_e1, d_c, d_yl, d_zp, d_zm, d_diag):
         pl.semaphore_signal(barrier, inc=1, device_id=target, device_id_type=MESH)
 
-    @pl.when(jnp.logical_not(is_self))
+    @pl.when(moved)
     def _():
-        pl.semaphore_signal(barrier, inc=1, device_id=d_perm, device_id_type=MESH)
-
+        pl.semaphore_signal(barrier, inc=1, device_id=d_xz, device_id_type=MESH)
+
+    @pl.when(turn)
+    def _():
+        pl.semaphore_signal(barrier, inc=1, device_id=d_turn, device_id_type=MESH)
+
+    loads[0].wait()
     half = xq.shape[1] // 2
     for j in range(2):
         part = xq[:, j * half:(j + 1) * half].astype(F32).T * xs[j:j + 1, :].astype(F32)
@@ -129,7 +142,7 @@
 
     pick[...] = picker(yh)
 
-    pl.semaphore_wait(barrier, jnp.where(is_self, 8, 9))
+    pl.semaphore_wait(barrier, 8 + jnp.where(moved, 1, 0) + jnp.where(turn, 1, 0))
 
     def place(zz, core, first, count):
         d_ = jnp.where(zz // 2 == xp, 1, 0)
@@ -137,21 +150,49 @@
         off = pl.multiple_of((k_ * 2 + first) * ROWS, ROWS)
         return aall.at[d_, core, :, pl.ds(off, count * ROWS)]
 
-    @pl.when(is_self)
+    def half_rows(zz, first, h):
+        d_ = jnp.where(zz // 2 == xp, 1, 0)
+        k_ = jnp.where(jnp.logical_or(zz == x, zz == 3 - x), 0, 1)
+        off = pl.multiple_of((k_ * 2 + first) * ROWS, ROWS)
+        return aall.at[d_, c, pl.ds(h * 128, 128), pl.ds(off, ROWS)]
+
+    halves = [pl.ds(h * 128, 128) for h in range(2)]
+    stays = jnp.logical_and(member, jnp.logical_not(turn))
+
+    @pl.when(stays)
     def _():
         local = pltpu.make_async_copy(x_own, place(z, c, yl, 1), lsem.at[4])
         local.start()
         local.wait()
 
-    @pl.when(jnp.logical_not(is_self))
+    @pl.when(jnp.logical_and(member, turn))
     def _():
-        send(x_own, place(z, c, yh, 1), I_PERM, d_perm)
+        for h in range(2):
+            send(x_own.at[halves[h]], half_rows(z, yh, h), I_PERM + h, d_turn)
+
+    @pl.when(jnp.logical_and(moved, jnp.logical_not(turn)))
+    def _():
+        for h in range(2):
+            send(x_own.at[halves[h]], half_rows(z, yl, h), I_PERM + h, d_xz)
+
+    @pl.when(jnp.logical_and(moved, turn))
+    def _():
+        for h in range(2):
+            send(x_own.at[halves[h]], x_way.at[halves[h]], I_WAY + h, d_xz)
+
+    def turn_way(h):
+        @pl.when(jnp.logical_and(moved, turn))
+        def _():
+            got(x_way.at[halves[h]], I_WAY + h)
+            send(x_way.at[halves[h]], half_rows(z, yh, h), I_PERM + h, d_turn)
 
     send(sel.at[yh], sel.at[yh], S_ALL, d_y)
     send(sel.at[yh], sel.at[2 + yh], S_ALL + 1, d_e0)
     send(sel.at[yh], sel.at[2 + yh], S_ALL + 2, d_diag)
 
     onehot_t = (ids[...] == lax.broadcasted_iota(jnp.int32, (32, ROWS), 0)).astype(F32)
+    for load in loads[1:]:
+        load.wait()
     gin_in[:, :UD] = feats[...]
     gin_in[:, UD:] = nn(onehot_t.T.astype(BF16), table[...]).astype(BF16)
     a_pre = nn(gin_in[...], ga[...])
@@ -160,8 +201,9 @@
     act[1] = a_act.T.astype(BF16)
     a_back[...] = jnp.zeros_like(a_back)
     mask = mask_row.T[:, 0:1]
-    sz_copy.wait()
-    og_copy.wait()
+
+    def send_e0(n):
+        send(zc.at[packed(yh), cols(n)], zc.at[packed(2 + yh), cols(n)], Z_E0 + n, d_e0)
 
     def first(k, carry):
         cc = cols(k)
@@ -173,30 +215,29 @@
         zfull[:, cc] = zk
         zc[packed(yh), cc] = nn(pick[...], zk).astype(BF16)
 
-        @pl.when(k < 4)
-        def _():
-            send(zc.at[packed(yh), cc], zc.at[packed(2 + yh), cc], Z_E0 + k, d_e0)
-
-        @pl.when(k == 5)
-        def _():
-            @pl.when(jnp.logical_not(is_self))
+        for h, at in enumerate((1, 3)):
+
+            @pl.when(k == at)
             def _():
-                got(place(z, c, yl, 1), I_PERM)
-
-            mine = place(z, c, yl, 1)
-            send(mine, mine, I_YL, d_yl)
-            send(mine, mine, I_Z1, d_zp)
-            send(mine, mine, I_Z1 + 1, d_zm)
-
-            def early(n, carry):
-                send(zc.at[packed(yh), cols(n)], zc.at[packed(yh), cols(n)], Z_Y + n, d_y)
-                return carry
-
-            lax.fori_loop(0, 5, early, 0)
-
-        @pl.when(k >= 5)
-        def _():
-            send(zc.at[packed(yh), cc], zc.at[packed(yh), cc], Z_Y + k, d_y)
+                turn_way(h)
+
+        for h, at in enumerate((3, 5)):
+
+            @pl.when(k == at)
+            def _():
+                mine = half_rows(z, yl, h)
+
+                @pl.when(jnp.logical_not(stays))
+                def _():
+                    got(mine, I_PERM + h)
+
+                send(mine, mine, I_YL + h, d_yl)
+                send(mine, mine, I_Z1 + 2 * h, d_zp)
+                send(mine, mine, I_Z1 + 2 * h + 1, d_zm)
+
+        @pl.when(k < FIRST)
+        def _():
+            send_e0(k)
 
         u = (jnp.maximum(pre, 0.0) * mg * (1.0 - 0.5 * gate)).astype(BF16)
         part = nn(act[1], u).astype(BF16)
@@ -209,6 +250,40 @@
         return carry
 
     lax.fori_loop(0, STEPS, first, 0)
+
+    zn, zb, zf = (z + 1) % 4, (z + 3) % 4, (z + 2) % 4
+
+    def z_low(n, first):
+        low = half_rows(zb, first, 0)
+        got(low, I_Z1 + 4 * n)
+        send(low, low, I_Z2 + 2 * n, d_zp)
+
+    def z_high(n, first):
+        high = half_rows(zn, first, 1)
+        got(high, I_Z1 + 4 * n + 3)
+        send(high, high, I_Z2 + 2 * n + 1, d_zm)
+
+    def z_rest(n, first):
+        got(half_rows(zn, first, 0), I_Z1 + 4 * n + 1)
+        got(half_rows(zb, first, 1), I_Z1 + 4 * n + 2)
+
+    def to_core(zz, i):
+        mine = place(zz, c, 0, 2)
+        send(mine, mine, I_CORE + i, d_c)
+
+    def from_y(h):
+        near = half_rows(z, 1 - yl, h)
+        got(near, I_YL + h)
+        send(near, near, I_Z1 + 4 + 2 * h, d_zp)
+        send(near, near, I_Z1 + 4 + 2 * h + 1, d_zm)
+
+    def send_y(n, carry):
+        send(zc.at[packed(yh), cols(n)], zc.at[packed(yh), cols(n)], Z_Y + n, d_y)
+        return carry
+
+    from_y(0)
+    lax.fori_loop(0, 2, send_y, 0)
+    z_low(0, yl)
 
     a_grad = jnp.where(act[0].astype(F32) > 0, a_back[...], 0.0).astype(BF16)
     part = nn(gin_in[...].astype(F32).T.astype(BF16), a_grad).astype(BF16)
@@ -223,31 +298,18 @@
         onehot_t, scen, (((1,), (0,)), ((), ())), precision=lax.Precision.HIGHEST, preferred_element_type=F32)
     over = jnp.maximum(jnp.sum(mask_row, axis=1, keepdims=True) - CAP, 0.0)
     tsend[0, 32:] = jnp.broadcast_to(over, (8, 128))
-    t_partners = (d_c, dev(yh, x, yl, z0, c), dev(yh, x, yl, 3 - z, c), d_yl, d_y, d_e1, d_e0)
+    t_partners = (d_c, dev(yh, x, yl, z0, c), dev(yh, x, yl, 3 - z, c), d_e1, d_e0, d_yl, d_y)
     send(tsend.at[0], trecv.at[0], T_ALL, t_partners[0])
 
     def user_rows(t):
         rows = gint[pl.ds(pl.multiple_of(t * USER, 8), USER), :]
         return jnp.concatenate([rows, jnp.zeros((XB - 256 - USER, ROWS), F32)], axis=0).astype(BF16)
 
-    zn, zb, zf = (z + 1) % 4, (z + 3) % 4, (z + 2) % 4
-
-    def half_rows(zz, first, h):
-        d_ = jnp.where(zz // 2 == xp, 1, 0)
-        k_ = jnp.where(jnp.logical_or(zz == x, zz == 3 - x), 0, 1)
-        off = pl.multiple_of((k_ * 2 + first) * ROWS, ROWS)
-        return aall.at[d_, c, pl.ds(h * 128, 128), pl.ds(off, ROWS)]
-
-    def z_forward(n, first):
-        got(place(zb, c, first, 1), I_Z1 + 2 * n)
-        got(place(zn, c, first, 1), I_Z1 + 2 * n + 1)
-        low, high = half_rows(zb, first, 0), half_rows(zn, first, 1)
-        send(low, low, I_Z2 + 2 * n, d_zp)
-        send(high, high, I_Z2 + 2 * n + 1, d_zm)
-
-    def to_core(zz, i):
-        mine = place(zz, c, 0, 2)
-        send(mine, mine, I_CORE + i, d_c)
+    from_y(1)
+
+    lax.fori_loop(2, STEPS, send_y, 0)
+    to_core(z, 0)
+    z_high(0, yl)
 
     def x_block(k, carry):
         wcopy(k).wait()
@@ -265,60 +327,39 @@
 
         return carry
 
-    def second(k):
+    def inputs_z2():
+        for n, first in enumerate((yl, 1 - yl)):
+            got(half_rows(zf, first, 0), I_Z2 + 2 * n)
+            got(half_rows(zf, first, 1), I_Z2 + 2 * n + 1)
+        to_core(zf, 3)
+
+    def forward(k):
         cc = cols(k)
-
-        @pl.when(k < 4)
-        def _():
-            lax.fori_loop(2 * k, 2 * k + 2, x_block, 0)
-
-        @pl.when(k == 0)
-        def _():
-            got(place(z, c, 1 - yl, 1), I_YL)
-            mine = place(z, c, 1 - yl, 1)
-            send(mine, mine, I_Z1 + 2, d_zp)
-            send(mine, mine, I_Z1 + 3, d_zm)
-            to_core(z, 0)
-            z_forward(0, yl)
-
-        @pl.when(k == 1)
-        def _():
-            z_forward(1, 1 - yl)
-            to_core(zb, 1)
-            to_core(zn, 2)
-
-        @pl.when(k == 2)
-        def _():
-            for n, first in enumerate((yl, 1 - yl)):
-                got(half_rows(zf, first, 0), I_Z2 + 2 * n)
-                got(half_rows(zf, first, 1), I_Z2 + 2 * n + 1)
-            to_core(zf, 3)
-
         got(zc.at[packed(1 - yh), cc], Z_Y + k)
         send(zc.at[packed(1 - yh), cc], zc.at[packed(3 - yh), cc], Z_FW + k, d_e0)
 
-        @pl.when(k < 4)
-        def _():
-            more = cols(k + 4)
-            send(zc.at[packed(yh), more], zc.at[packed(2 + yh), more], Z_E0 + 4 + k, d_e0)
+        @pl.when(jnp.logical_and(k >= 4, k < 6))
+        def _():
+            send_e0(k + 2)
 
     def table_step(s):
         got(trecv.at[s - 1], T_ALL + s - 1)
         tsend[s] = tsend[s - 1] + trecv[s - 1]
         send(tsend.at[s], trecv.at[s], T_ALL + s, t_partners[s])
 
-    def pack_inputs():
+    def wait_inputs():
         for i, zz in enumerate((z, zb, zn, zf)):
             got(place(zz, 1 - c, 0, 2), I_CORE + i)
         got(sel.at[1 - yh], S_ALL)
         got(sel.at[2 + yh], S_ALL + 1)
         got(sel.at[3 - yh], S_ALL + 2)
+
+    def pack_inputs(d_):
         for s in range(4):
             p = picker(s)
-            for d_ in range(2):
-                for j in range(2):
-                    ac[d_, j, :, s * CAP:(s + 1) * CAP] = nt(
-                        aall[d_, j, :, s * ROWS:(s + 1) * ROWS], p).astype(BF16)
+            for j in range(2):
+                ac[d_, j, :, s * CAP:(s + 1) * CAP] = nt(
+                    aall[d_, j, :, s * ROWS:(s + 1) * ROWS], p).astype(BF16)
 
     def core_sum():
         def one(n, carry):
@@ -388,26 +429,30 @@
 
     extra = {
         1: (table_at(1),),
-        3: (table_at(2),),
-        4: (core_sum,),
-        5: (table_at(3), x_z1, gate_e1),
-        7: (table_at(4),),
-        8: (table_at(5), x_z2),
-        9: (table_at(6), gate_y),
-        10: (x_last,),
-        11: (table_last, gate_e0),
+        2: (table_at(2),),
+        3: (core_sum, table_at(3)),
+        5: (gate_e1,),
+        6: (x_z1, table_at(4)),
+        8: (table_at(5),),
+        9: (x_z2, gate_y, table_at(6)),
+        11: (x_last, gate_e0, table_last),
     }
 
+    def main_copy(n):
+        return pltpu.make_async_copy(main_v.at[:, cols(n)], main_out.at[:, cols(n)], lsem.at[9 + n])
+
     def step(i, carry):
-        @pl.when(i < STEPS)
-        def _():
-            second(i)
+        j = i - LAG
+
+        @pl.when(i == 1)
+        def _():
+            forward(1)
+            inputs_z2()
 
         @pl.when(i == LAG)
         def _():
-            pack_inputs()
-
-        j = i - LAG
+            wait_inputs()
+            pack_inputs(0)
 
         @pl.when(jnp.logical_and(j >= 0, j < STEPS))
         def _():
@@ -418,6 +463,35 @@
                 ps[h * 256:(h + 1) * 256, cc] = nn(ac[0, h], zc[:, cc]).astype(BF16)
             send(ps.at[:, cc], pr.at[:, cc], M_E1 + j, d_e1)
 
+        @pl.when(i == LAG)
+        def _():
+            pack_inputs(1)
+
+        @pl.when(i < 4)
+        def _():
+            lax.fori_loop(2 * i, 2 * i + 2, x_block, 0)
+
+        @pl.when(i == 0)
+        def _():
+            z_low(1, 1 - yl)
+            z_high(1, 1 - yl)
+            for n, first in enumerate((yl, 1 - yl)):
+                z_rest(n, first)
+            to_core(zb, 1)
+            to_core(zn, 2)
+
+        @pl.when(i < 2)
+        def _():
+            forward(2 * i)
+
+        @pl.when(jnp.logical_and(i >= 2, i < 5))
+        def _():
+            forward(2 * i - 1)
+
+            @pl.when(i < 4)
+            def _():
+                forward(2 * i)
+
         for at, calls in extra.items():
 
             @pl.when(i == at)
@@ -425,20 +499,22 @@
                 for call in calls:
                     call()
 
-        @pl.when(jnp.logical_and(j >= 1, j <= STEPS))
-        def _():
-            cc = cols(j - 1)
-            got(pr.at[:, cc], M_E1 + j - 1)
+        @pl.when(j >= AHEAD)
+        def _():
+            cc = cols(j - AHEAD)
+            got(pr.at[:, cc], M_E1 + j - AHEAD)
             for h in range(2):
                 total = pr[h * 256:(h + 1) * 256, cc].astype(F32) + nn(ac[1, h], zc[:, cc])
-                main_out[h * 256:(h + 1) * 256, cc] = total.astype(BF16)
+                main_v[h * 256:(h + 1) * 256, cc] = total.astype(BF16)
+            main_copy(j - AHEAD).start()
 
         return carry
 
-    lax.fori_loop(0, STEPS + LAG + 1, step, 0)
+    lax.fori_loop(0, STEPS + LAG + AHEAD, step, 0)
 
     def drain(k, carry):
         cc = cols(k)
+        main_copy(k).wait()
         sent(zc.at[packed(0), cc], Z_Y + k)
         sent(zc.at[packed(0), cc], Z_E0 + k)
         sent(zc.at[packed(0), cc], Z_FW + k)
@@ -452,13 +528,21 @@
     sent(gr2, G_Y)
     sent(gr3, G_E0)
 
-    @pl.when(jnp.logical_not(is_self))
+    @pl.when(jnp.logical_not(stays))
     def _():
-        sent(x_own, I_PERM)
-
-    sent(place(z, c, 0, 1), I_YL)
+        for h in range(2):
+            sent(x_own.at[halves[h]], I_PERM + h)
+
+    @pl.when(jnp.logical_and(moved, turn))
+    def _():
+        for h in range(2):
+            sent(x_own.at[halves[h]], I_WAY + h)
+
+    for i in range(2):
+        sent(half_rows(z, 0, 0), I_YL + i)
+    for i in range(8):
+        sent(half_rows(z, 0, 0), I_Z1 + i)
     for i in range(4):
-        sent(place(z, c, 0, 1), I_Z1 + i)
         sent(half_rows(z, 0, 0), I_Z2 + i)
     for i in range(2):
         sent(xz1.at[i], X_Z1 + i)
@@ -472,19 +556,31 @@
         sent(tsend.at[s], T_ALL + s)
 
 
-def copy_kernel(*refs):
-    n = len(refs) // 2
-    for i in range(n):
-        refs[n + i][...] = refs[i][...]
+def copy_kernel(n, *refs):
+    held, into, out = refs[2 * n:3 * n], refs[3 * n], refs[3 * n + 1]
+    parts = [(i, slice(None)) for i in range(1, n)]
+    parts += [(0, pl.ds(r, 64)) for r in range(0, 512, 64)]
+    first = [pltpu.make_async_copy(refs[i].at[r], held[i].at[r], into.at[p]) for p, (i, r) in enumerate(parts)]
+    second = [pltpu.make_async_copy(held[i].at[r], refs[n + i].at[r], out.at[p]) for p, (i, r) in enumerate(parts)]
+    for copy in first:
+        copy.start()
+    for one, two in zip(first, second):
+        one.wait()
+        two.start()
+    for copy in second:
+        copy.wait()
 
 
 def copy_out(*arrays):
-    vmem = pl.BlockSpec(memory_space=pltpu.VMEM)
+    hbm = pl.BlockSpec(memory_space=pl.ANY)
+    n = len(arrays)
     return pl.pallas_call(
-        copy_kernel,
+        functools.partial(copy_kernel, n),
         out_shape=tuple(jax.ShapeDtypeStruct(a.shape, a.dtype) for a in arrays),
-        in_specs=[vmem] * len(arrays),
-        out_specs=(vmem,) * len(arrays),
+        in_specs=[hbm] * n,
+        out_specs=(hbm,) * n,
+        scratch_shapes=[pltpu.VMEM(a.shape, a.dtype) for a in arrays]
+        + [pltpu.SemaphoreType.DMA((n + 7,)), pltpu.SemaphoreType.DMA((n + 7,))],
     )(*arrays)
 
 
@@ -525,9 +621,13 @@
             jax.ShapeDtypeStruct((32, 128), F32),
             jax.ShapeDtypeStruct((1, 1), F32),
         ),
-        in_specs=[vmem] * 8 + [hbm] * 3,
-        out_specs=(vmem,) * 6 + (pl.BlockSpec(memory_space=pltpu.SMEM),),
+        in_specs=[vmem] * 4 + [hbm] * 7,
+        out_specs=(hbm,) + (vmem,) * 5 + (pl.BlockSpec(memory_space=pltpu.SMEM),),
         scratch_shapes=[
+            pltpu.VMEM((ROWS, 256), BF16),
+            pltpu.VMEM((ROWS, UD), BF16),
+            pltpu.VMEM((GH, GH), BF16),
+            pltpu.VMEM((GH, H), BF16),
             pltpu.VMEM((ROWS, H), BF16),
             pltpu.VMEM((ROWS, H), BF16),
             pltpu.VMEM((2, 512, H), BF16),
@@ -539,6 +639,7 @@
             pltpu.VMEM((512, ROWS), F32),
             pltpu.VMEM((2, 2, 256, 4 * ROWS), BF16),
             pltpu.VMEM((2, 2, 256, DEPTH), BF16),
+            pltpu.VMEM((256, ROWS), BF16),
             pltpu.VMEM((256, ROWS), BF16),
             pltpu.VMEM((CAP, ROWS), BF16),
             pltpu.VMEM((4, 8, ROWS), F32),
@@ -555,9 +656,10 @@
             pltpu.VMEM((XB, ROWS), BF16),
             pltpu.VMEM((512, H), BF16),
             pltpu.VMEM((512, H), BF16),
+            pltpu.VMEM((512, H), BF16),
             pltpu.VMEM((7, 40, 128), F32),
             pltpu.VMEM((7, 40, 128), F32),
-            pltpu.SemaphoreType.DMA((5,)),
+            pltpu.SemaphoreType.DMA((9 + STEPS,)),
             pltpu.SemaphoreType.DMA((N_SEM,)),
             pltpu.SemaphoreType.DMA((N_SEM,)),
         ],
@@ -565,8 +667,8 @@
             collective_id=0, has_side_effects=True, vmem_limit_bytes=60 * 1024 * 1024),
         cost_estimate=pl.CostEstimate(flops=21_000_000_000, bytes_accessed=28_000_000, transcendentals=1_000_000),
     )(
-        x_quant, x_scale.T, user_feats, scenario_ids[None, :], scenario_table,
-        label_mask.T, gate_a[0], gate_b[0], saved_z[0], out_grad[0], main_weight[0],
+        x_scale.T, scenario_ids[None, :], scenario_table, label_mask.T, x_quant, user_feats, gate_a[0], gate_b[0],
+        saved_z[0], out_grad[0], main_weight[0],
     )
     main, grad_a, grad_b, x_grad, user, table_grad = copy_out(*outs[:6])
     args = (

time: 105 us -> 97.3 us (0.927)
  Pallas kernels: 103 us -> 94.1 us
    pallas_call x1, Pallas kernels: 99.5 us -> 91.4 us  [body(): pl.pallas_call(kernel, out_shape=(jax.ShapeDtypeStruct((512, H), BF16), j...]
where the time goes in v3:
time: 97.3 us; the launch traced here: 95.9 us
  Pallas kernels  94.1 us (97%)
    pallas_call x1, Pallas kernels, body(): pl.pallas_call(kernel, out_shape=(jax.ShapeDtypeStruct((512, H), BF16), j...  91.4 us
    pallas_call x1, Pallas kernels, copy_out(): pl.pallas_call(functools.partial(copy_kernel, n), out_shape=tuple((jax.Sh...  2.71 us

profile of v3, /device:TPU:8, one launch (start us, length us, event | category | flops | bytes accessed | tf_op | source)
XLA Modules:
  0.0 95.9 jit_solution(9543920460487141310)
XLA Ops:
  0.6 0.0 copy-start
  0.6 0.0 copy-start.1
  0.7 0.0 copy-start.2
  0.7 0.0 copy-start.3
  0.7 0.0 copy-start.4
  0.7 0.0 copy-start.5
  0.7 0.0 copy-start.6
  0.7 91.4 %shard_map.154 = (bf16[512,2048]{1,0:T(8,128)(2,1)}, bf16[64,512]{1,0:T(8,128)(2,1)}, bf16[64,2048]{1,0:T(8,128)(2,1)}, bf16[512,256]{1,0:T(8,128)(2,1)}, bf16[2...) custom-call(bf16[2,512]{1,0:T(2,128)(2,1)} %bitcast.47, s32[1,512]{1,0:T(1,128)} %bitcast.46, ...), custom_call_target="tpu_custom_call" | custom-call | flops 20999999488 | bytes 28000000 | tf_op jit(solution)/shard_map/pallas_call | solution.py:613
  92.1 2.7 %shard_map.155 = (bf16[512,2048]{1,0:T(8,128)(2,1)}, bf16[64,512]{1,0:T(8,128)(2,1)}, bf16[64,2048]{1,0:T(8,128)(2,1)}, bf16[512,256]{1,0:T(8,128)(2,1)}, bf16[24,512]{1,0:T(8,128)(2,1)}, /*index=5*/f32[32,128]{1,0:T(8,128)}) custom-call(bf16[512,2048]{1,0:T(8,128)(2,1)} %get-tuple-element.80.refs_0_, bf16[64,512]{1,0:T(8,128)(2,1)} %get-tuple-element.81.refs_1_, ...), custom_call_target="tpu_custom_call" | custom-call | tf_op jit(solution)/shard_map/pallas_call | solution.py:577
  94.8 0.0 copy-done
  94.8 0.1 copy.17
  95.0 0.0 copy-done.1
  95.0 0.0 copy-done.2
  95.0 0.0 copy-done.3
  95.0 0.0 copy-done.4
  95.0 0.0 copy-done.5
  95.0 0.0 copy-done.6
  95.0 0.8 while.9
Async XLA Ops:
  0.6 94.2 %copy-start = (bf16[512,256]{1,0:T(8,128)(2,1)S(1)}, bf16[512,256]{1,0:T(8,128)(2,1)}, u32[]{:S(2)}) copy-start(bf16[512,256]{1,0:T(8,128)(2,1)} %xq_hbm.1) | copy-start | bytes 786436
  0.6 94.3 %copy-start.1 = (bf16[32,128]{1,0:T(8,128)(2,1)S(1)}, bf16[32,128]{1,0:T(8,128)(2,1)}, u32[]{:S(2)}) copy-start(bf16[32,128]{1,0:T(8,128)(2,1)} %table.1) | copy-start | bytes 24580
  0.7 94.3 %copy-start.2 = (s32[512]{0:T(512)S(1)}, s32[512]{0:T(512)}, u32[]{:S(2)}) copy-start(s32[512]{0:T(512)} %param.16) | copy-start | bytes 6148
  0.7 94.3 %copy-start.3 = (bf16[512,2]{0,1:T(2,128)(2,1)S(1)}, bf16[512,2]{0,1:T(2,128)(2,1)}, u32[]{:S(2)}) copy-start(bf16[512,2]{0,1:T(2,128)(2,1)} %param.14) | copy-start | bytes 6148
  0.7 94.3 %copy-start.4 = (s32[512,1]{0,1:T(1,128)S(1)}, s32[512,1]{0,1:T(1,128)}, u32[]{:S(2)}) copy-start(s32[512,1]{0,1:T(1,128)} %param.18) | copy-start | bytes 6148
  0.7 94.3 %copy-start.5 = (bf16[1,512,2048]{2,1,0:T(8,128)(2,1)S(1)}, bf16[1,512,2048]{2,1,0:T(8,128)(2,1)}, u32[]{:S(2)}) copy-start(bf16[1,512,2048]{2,1,0:T(8,128)(2,1)} %param.23) | copy-start | bytes 6291460
  0.7 94.3 %copy-start.6 = (bf16[1,512,512]{2,1,0:T(8,128)(2,1)S(1)}, bf16[1,512,512]{2,1,0:T(8,128)(2,1)}, u32[]{:S(2)}) copy-start(bf16[1,512,512]{2,1,0:T(8,128)(2,1)} %param.22) | copy-start | bytes 1572868

commit v4 on v3

--- a/solution.py
+++ b/solution.py
@@ -21,7 +21,7 @@
 USER = 24
 CAP = 320
 DEPTH = 4 * CAP
-FIRST = 6
+FIRST = 4
 AHEAD = 2
 LAG = 2
 
@@ -205,8 +205,21 @@
     def send_e0(n):
         send(zc.at[packed(yh), cols(n)], zc.at[packed(2 + yh), cols(n)], Z_E0 + n, d_e0)
 
+    relay = jnp.logical_and(moved, turn)
+
+    def arrived(h):
+        mine = half_rows(z, yl, h)
+
+        @pl.when(jnp.logical_not(stays))
+        def _():
+            got(mine, I_PERM + h)
+
+        send(mine, mine, I_YL + h, d_yl)
+        send(mine, mine, I_Z1 + 2 * h, d_zp)
+        send(mine, mine, I_Z1 + 2 * h + 1, d_zm)
+
     def first(k, carry):
-        cc = cols(k)
+        cc = pl.ds(pl.multiple_of(k * 2 * CH, 2 * CH), 2 * CH)
         gate = 2.0 * jax.nn.sigmoid(nn(act[0], gb[:, cc]))
         masked = og[:, cc].astype(F32) * mask
         pre = sz[:, cc].astype(F32)
@@ -214,42 +227,36 @@
         zk = jnp.where(pre > 0, mg, 0.0).astype(BF16)
         zfull[:, cc] = zk
         zc[packed(yh), cc] = nn(pick[...], zk).astype(BF16)
-
-        for h, at in enumerate((1, 3)):
-
-            @pl.when(k == at)
-            def _():
-                turn_way(h)
-
-        for h, at in enumerate((3, 5)):
-
-            @pl.when(k == at)
-            def _():
-                mine = half_rows(z, yl, h)
-
-                @pl.when(jnp.logical_not(stays))
-                def _():
-                    got(mine, I_PERM + h)
-
-                send(mine, mine, I_YL + h, d_yl)
-                send(mine, mine, I_Z1 + 2 * h, d_zp)
-                send(mine, mine, I_Z1 + 2 * h + 1, d_zm)
-
-        @pl.when(k < FIRST)
-        def _():
-            send_e0(k)
-
         u = (jnp.maximum(pre, 0.0) * mg * (1.0 - 0.5 * gate)).astype(BF16)
         part = nn(act[1], u).astype(BF16)
         for i in range(2):
             for j in range(2):
                 r = (i * 2 + j) * 128
                 gpart[i, j, :, cc] = part[r:r + 128]
-        send(gpart.at[:, 1 - xp, :, cc], gr1.at[:, :, cc], G_E1 + k, d_e1)
         a_back[...] += nt(u, gb[:, cc])
+
+        @pl.when(k < FIRST // 2)
+        def _():
+            send_e0(2 * k)
+            send_e0(2 * k + 1)
+
+        for h in range(2):
+            one = cols(2 * k + h)
+            send(gpart.at[:, 1 - xp, :, one], gr1.at[:, :, one], G_E1 + 2 * k + h, d_e1)
+
+        for h in range(2):
+
+            @pl.when(k == h)
+            def _():
+                turn_way(h)
+
+            @pl.when(k == jnp.where(relay, h + 2, h + 1))
+            def _():
+                arrived(h)
+
         return carry
 
-    lax.fori_loop(0, STEPS, first, 0)
+    lax.fori_loop(0, STEPS // 2, first, 0)
 
     zn, zb, zf = (z + 1) % 4, (z + 3) % 4, (z + 2) % 4
 
@@ -338,7 +345,7 @@
         got(zc.at[packed(1 - yh), cc], Z_Y + k)
         send(zc.at[packed(1 - yh), cc], zc.at[packed(3 - yh), cc], Z_FW + k, d_e0)
 
-        @pl.when(jnp.logical_and(k >= 4, k < 6))
+        @pl.when(jnp.logical_and(k >= 2, k < 6))
         def _():
             send_e0(k + 2)
 
@@ -430,7 +437,8 @@
     extra = {
         1: (table_at(1),),
         2: (table_at(2),),
-        3: (core_sum, table_at(3)),
+        3: (table_at(3),),
+        4: (core_sum, lambda: pack_inputs(1)),
         5: (gate_e1,),
         6: (x_z1, table_at(4)),
         8: (table_at(5),),
@@ -446,8 +454,14 @@
 
         @pl.when(i == 1)
         def _():
-            forward(1)
+            def x_and_forward(n, carry):
+                x_block(n + 2, carry)
+                forward(n)
+                return carry
+
+            lax.fori_loop(0, 2, x_and_forward, 0)
             inputs_z2()
+            forward(2)
 
         @pl.when(i == LAG)
         def _():
@@ -463,11 +477,15 @@
                 ps[h * 256:(h + 1) * 256, cc] = nn(ac[0, h], zc[:, cc]).astype(BF16)
             send(ps.at[:, cc], pr.at[:, cc], M_E1 + j, d_e1)
 
-        @pl.when(i == LAG)
-        def _():
-            pack_inputs(1)
-
-        @pl.when(i < 4)
+        @pl.when(jnp.logical_and(i >= 2, i < 5))
+        def _():
+            @pl.when(i > 2)
+            def _():
+                forward(2 * i - 2)
+
+            forward(2 * i - 1)
+
+        @pl.when(jnp.logical_and(i < 4, i != 1))
         def _():
             lax.fori_loop(2 * i, 2 * i + 2, x_block, 0)
 
@@ -479,18 +497,6 @@
                 z_rest(n, first)
             to_core(zb, 1)
             to_core(zn, 2)
-
-        @pl.when(i < 2)
-        def _():
-            forward(2 * i)
-
-        @pl.when(jnp.logical_and(i >= 2, i < 5))
-        def _():
-            forward(2 * i - 1)
-
-            @pl.when(i < 4)
-            def _():
-                forward(2 * i)
 
         for at, calls in extra.items():
 

time: 97.3 us -> 96.6 us (level); the launches traced: 95.9 us -> 96.4 us
  no operation moved by 1% of the time
where the time goes in v4:
time: 96.6 us; the launch traced here: 96.4 us
  Pallas kernels  94.5 us (98%)
    pallas_call x1, Pallas kernels, body(): pl.pallas_call(kernel, out_shape=(jax.ShapeDtypeStruct((512, H), BF16), j...  91.8 us
    pallas_call x1, Pallas kernels, copy_out(): pl.pallas_call(functools.partial(copy_kernel, n), out_shape=tuple((jax.Sh...  2.71 us

profile of v4, /device:TPU:8, one launch (start us, length us, event | category | flops | bytes accessed | tf_op | source)
XLA Modules:
  0.0 96.4 jit_solution(4715130716636250520)
XLA Ops:
  0.6 0.0 copy-start
  0.6 0.0 copy-start.1
  0.7 0.0 copy-start.2
  0.7 0.0 copy-start.3
  0.7 0.0 copy-start.4
  0.7 0.0 copy-start.5
  0.7 0.0 copy-start.6
  0.7 91.8 %shard_map.154 = (bf16[512,2048]{1,0:T(8,128)(2,1)}, bf16[64,512]{1,0:T(8,128)(2,1)}, bf16[64,2048]{1,0:T(8,128)(2,1)}, bf16[512,256]{1,0:T(8,128)(2,1)}, bf16[2...) custom-call(bf16[2,512]{1,0:T(2,128)(2,1)} %bitcast.47, s32[1,512]{1,0:T(1,128)} %bitcast.46, ...), custom_call_target="tpu_custom_call" | custom-call | flops 20999999488 | bytes 28000000 | tf_op jit(solution)/shard_map/pallas_call | solution.py:619
  92.5 2.7 %shard_map.155 = (bf16[512,2048]{1,0:T(8,128)(2,1)}, bf16[64,512]{1,0:T(8,128)(2,1)}, bf16[64,2048]{1,0:T(8,128)(2,1)}, bf16[512,256]{1,0:T(8,128)(2,1)}, bf16[24,512]{1,0:T(8,128)(2,1)}, /*index=5*/f32[32,128]{1,0:T(8,128)}) custom-call(bf16[512,2048]{1,0:T(8,128)(2,1)} %get-tuple-element.80.refs_0_, bf16[64,512]{1,0:T(8,128)(2,1)} %get-tuple-element.81.refs_1_, ...), custom_call_target="tpu_custom_call" | custom-call | tf_op jit(solution)/shard_map/pallas_call | solution.py:583
  95.3 0.0 copy-done
  95.3 0.1 copy.17
  95.4 0.0 copy-done.1
  95.4 0.0 copy-done.2
  95.4 0.0 copy-done.3
  95.4 0.0 copy-done.4
  95.5 0.0 copy-done.5
  95.5 0.0 copy-done.6
  95.5 0.8 while.9
Async XLA Ops:
  0.6 94.6 %copy-start = (bf16[512,256]{1,0:T(8,128)(2,1)S(1)}, bf16[512,256]{1,0:T(8,128)(2,1)}, u32[]{:S(2)}) copy-start(bf16[512,256]{1,0:T(8,128)(2,1)} %xq_hbm.1) | copy-start | bytes 786436
  0.6 94.8 %copy-start.1 = (bf16[32,128]{1,0:T(8,128)(2,1)S(1)}, bf16[32,128]{1,0:T(8,128)(2,1)}, u32[]{:S(2)}) copy-start(bf16[32,128]{1,0:T(8,128)(2,1)} %table.1) | copy-start | bytes 24580
  0.7 94.8 %copy-start.2 = (s32[512]{0:T(512)S(1)}, s32[512]{0:T(512)}, u32[]{:S(2)}) copy-start(s32[512]{0:T(512)} %param.16) | copy-start | bytes 6148
  0.7 94.8 %copy-start.3 = (bf16[512,2]{0,1:T(2,128)(2,1)S(1)}, bf16[512,2]{0,1:T(2,128)(2,1)}, u32[]{:S(2)}) copy-start(bf16[512,2]{0,1:T(2,128)(2,1)} %param.14) | copy-start | bytes 6148
  0.7 94.8 %copy-start.4 = (s32[512,1]{0,1:T(1,128)S(1)}, s32[512,1]{0,1:T(1,128)}, u32[]{:S(2)}) copy-start(s32[512,1]{0,1:T(1,128)} %param.18) | copy-start | bytes 6148
  0.7 94.8 %copy-start.5 = (bf16[1,512,2048]{2,1,0:T(8,128)(2,1)S(1)}, bf16[1,512,2048]{2,1,0:T(8,128)(2,1)}, u32[]{:S(2)}) copy-start(bf16[1,512,2048]{2,1,0:T(8,128)(2,1)} %param.23) | copy-start | bytes 6291460
  0.7 94.8 %copy-start.6 = (bf16[1,512,512]{2,1,0:T(8,128)(2,1)S(1)}, bf16[1,512,512]{2,1,0:T(8,128)(2,1)}, u32[]{:S(2)}) copy-start(bf16[1,512,512]{2,1,0:T(8,128)(2,1)} %param.22) | copy-start | bytes 1572868

commit v5 on v4

--- a/solution.py
+++ b/solution.py
@@ -455,8 +455,8 @@
         @pl.when(i == 1)
         def _():
             def x_and_forward(n, carry):
+                forward(n)
                 x_block(n + 2, carry)
-                forward(n)
                 return carry
 
             lax.fori_loop(0, 2, x_and_forward, 0)

time: 96.6 us -> 96.8 us (level); the launches traced: 96.4 us -> 95.5 us
  no operation moved by 1% of the time
where the time goes in v5:
time: 96.8 us; the launch traced here: 95.5 us
  Pallas kernels  93.7 us (97%)
    pallas_call x1, Pallas kernels, body(): pl.pallas_call(kernel, out_shape=(jax.ShapeDtypeStruct((512, H), BF16), j...  91 us
    pallas_call x1, Pallas kernels, copy_out(): pl.pallas_call(functools.partial(copy_kernel, n), out_shape=tuple((jax.Sh...  2.71 us

profile of v5, /device:TPU:8, one launch (start us, length us, event | category | flops | bytes accessed | tf_op | source)
XLA Modules:
  0.0 95.5 jit_solution(13854330751475345577)
XLA Ops:
  0.6 0.0 copy-start
  0.6 0.0 copy-start.1
  0.7 0.0 copy-start.2
  0.7 0.0 copy-start.3
  0.7 0.0 copy-start.4
  0.7 0.0 copy-start.5
  0.7 0.0 copy-start.6
  0.7 91.0 %shard_map.154 = (bf16[512,2048]{1,0:T(8,128)(2,1)}, bf16[64,512]{1,0:T(8,128)(2,1)}, bf16[64,2048]{1,0:T(8,128)(2,1)}, bf16[512,256]{1,0:T(8,128)(2,1)}, bf16[2...) custom-call(bf16[2,512]{1,0:T(2,128)(2,1)} %bitcast.47, s32[1,512]{1,0:T(1,128)} %bitcast.46, ...), custom_call_target="tpu_custom_call" | custom-call | flops 20999999488 | bytes 28000000 | tf_op jit(solution)/shard_map/pallas_call | solution.py:619
  91.7 2.7 %shard_map.155 = (bf16[512,2048]{1,0:T(8,128)(2,1)}, bf16[64,512]{1,0:T(8,128)(2,1)}, bf16[64,2048]{1,0:T(8,128)(2,1)}, bf16[512,256]{1,0:T(8,128)(2,1)}, bf16[24,512]{1,0:T(8,128)(2,1)}, /*index=5*/f32[32,128]{1,0:T(8,128)}) custom-call(bf16[512,2048]{1,0:T(8,128)(2,1)} %get-tuple-element.80.refs_0_, bf16[64,512]{1,0:T(8,128)(2,1)} %get-tuple-element.81.refs_1_, ...), custom_call_target="tpu_custom_call" | custom-call | tf_op jit(solution)/shard_map/pallas_call | solution.py:583
  94.4 0.0 copy-done
  94.4 0.1 copy.17
  94.6 0.0 copy-done.1
  94.6 0.0 copy-done.2
  94.6 0.0 copy-done.3
  94.6 0.0 copy-done.4
  94.6 0.0 copy-done.5
  94.6 0.0 copy-done.6
  94.6 0.8 while.9
Async XLA Ops:
  0.6 93.8 %copy-start = (bf16[512,256]{1,0:T(8,128)(2,1)S(1)}, bf16[512,256]{1,0:T(8,128)(2,1)}, u32[]{:S(2)}) copy-start(bf16[512,256]{1,0:T(8,128)(2,1)} %xq_hbm.1) | copy-start | bytes 786436
  0.6 93.9 %copy-start.1 = (bf16[32,128]{1,0:T(8,128)(2,1)S(1)}, bf16[32,128]{1,0:T(8,128)(2,1)}, u32[]{:S(2)}) copy-start(bf16[32,128]{1,0:T(8,128)(2,1)} %table.1) | copy-start | bytes 24580
  0.7 93.9 %copy-start.2 = (s32[512]{0:T(512)S(1)}, s32[512]{0:T(512)}, u32[]{:S(2)}) copy-start(s32[512]{0:T(512)} %param.16) | copy-start | bytes 6148
  0.7 93.9 %copy-start.3 = (bf16[512,2]{0,1:T(2,128)(2,1)S(1)}, bf16[512,2]{0,1:T(2,128)(2,1)}, u32[]{:S(2)}) copy-start(bf16[512,2]{0,1:T(2,128)(2,1)} %param.14) | copy-start | bytes 6148
  0.7 93.9 %copy-start.4 = (s32[512,1]{0,1:T(1,128)S(1)}, s32[512,1]{0,1:T(1,128)}, u32[]{:S(2)}) copy-start(s32[512,1]{0,1:T(1,128)} %param.18) | copy-start | bytes 6148
  0.7 93.9 %copy-start.5 = (bf16[1,512,2048]{2,1,0:T(8,128)(2,1)S(1)}, bf16[1,512,2048]{2,1,0:T(8,128)(2,1)}, u32[]{:S(2)}) copy-start(bf16[1,512,2048]{2,1,0:T(8,128)(2,1)} %param.23) | copy-start | bytes 6291460
  0.7 93.9 %copy-start.6 = (bf16[1,512,512]{2,1,0:T(8,128)(2,1)S(1)}, bf16[1,512,512]{2,1,0:T(8,128)(2,1)}, u32[]{:S(2)}) copy-start(bf16[1,512,512]{2,1,0:T(8,128)(2,1)} %param.22) | copy-start | bytes 1572868
